TPU v7x, 32 devices: a whole 2x2x4 slice. The times are simulated.
32 devices in a mesh: grp: 4 (over y, x), band: 8 (over z, core).
Axes of the slice: x: 2, y: 2, z: 4, core: 2. Of those that a mesh axis runs over, the one named last changes fastest.
Arguments:
- frames: bfloat16 [4, 5, 16, 2048], P('grp', None, 'band'), may hold values from -6 to 6
- grid_size: int32 [4, 2], P('grp'), may hold values from 1 to 128, as said below
- out_grad: bfloat16 [4, 15, 16, 16384], P('grp', None, 'band'), may hold values from -6 to 6
- enc_hidden: float32 [512, 1152], P('band'), may hold values from -0.3125 to 0.3125
- enc_hidden_m: float32 [512, 1152], P('band'), may hold values from -32 to 32
- enc_hidden_v: float32 [512, 1152], P('band'), may hold values from 18.432 to 9437.184
- fore_hidden: float32 [512, 1152], P('band'), may hold values from -0.3125 to 0.3125
- fore_hidden_m: float32 [512, 1152], P('band'), may hold values from -224 to 224
- fore_hidden_v: float32 [512, 1152], P('band'), may hold values from 614.4 to 9830.4
- enc_input: float32 [512, 144], P('band'), may hold values from -0.5 to 0.5
- enc_input_m: float32 [512, 144], P('band'), may hold values from -128 to 128
- enc_input_v: float32 [512, 144], P('band'), may hold values from 204.8 to 104857.6
- cell_vectors: float32 [1792], P('band'), as said below
- vectors_m: float32 [1792], P('band'), may hold values from -640 to 640
- vectors_v: float32 [1792], P('band'), may hold values from 5529.6 to 88473.6
Outputs:
- h_out: bfloat16 [4, 15, 16, 16384], P('grp', None, 'band')
- d_frames: float32 [4, 5, 16, 2048], P('grp', None, 'band')
- enc_hidden_new: float32 [512, 1152], P('band')
- enc_hidden_m_new: float32 [512, 1152], P('band')
- enc_hidden_v_new: float32 [512, 1152], P('band')
- enc_hidden_bf16: bfloat16 [512, 1152], P('band')
- fore_hidden_new: float32 [512, 1152], P('band')
- fore_hidden_m_new: float32 [512, 1152], P('band')
- fore_hidden_v_new: float32 [512, 1152], P('band')
- fore_hidden_bf16: bfloat16 [512, 1152], P('band')
- enc_input_new: float32 [512, 144], P('band')
- enc_input_m_new: float32 [512, 144], P('band')
- enc_input_v_new: float32 [512, 144], P('band')
- enc_input_bf16: bfloat16 [512, 144], P('band')
- vectors_new: float32 [1792], P('band')
- vectors_m_new: float32 [1792], P('band')
- vectors_v_new: float32 [1792], P('band')
- vectors_bf16: bfloat16 [1792], P('band')
Inputs may be any that keep to these rules, and one draw needn't show every extreme that they name: `grid_size`: row limit then column limit of each grid; 2 grids, drawn from the seed, have all 16 rows and 128 columns, the others between five and seven eighths of each. `cell_vectors`: for each of the two cells in turn: 128 biases for each of the gates i, f, g, o, then 128 peephole weights for each of i, f, o.
All inputs are finite; a program needn't handle non-finite values.
Results may differ from a plain program's by a relative error of at most 0.023.
Values may be sent and summed in bfloat16 or wider, within the bound.
No kernel may reach another device: no remote copies, remote signals or barrier semaphores. Data moves between devices by JAX's collectives and lax.ppermute only.
A program may use at most 64 MiB of HBM per device.

v0:
```python
import jax
import jax.numpy as jnp
from jax import lax
from jax.sharding import PartitionSpec as P

HID = 128
FRAMES_IN = 5
FRAMES_OUT = 15
STEP = 5


beta_first = 0.5
beta_second = 0.5
adam_epsilon = 1e-08
weight_decay = 0.01
matrix_rate = 0.03
vector_rate = 0.3


def from_behind(value, axis, steps):
    count = lax.axis_size(axis)
    first, last = (max(0, -steps), min(count, count - steps))
    return lax.ppermute(value, axis, [(source, source + steps) for source in range(first, last)])


def cut_along(array, dim, peers):
    shape = array.shape
    tiles = array.reshape(*shape[:dim], peers, shape[dim] // peers, *shape[dim + 1 :])
    return jnp.moveaxis(tiles, dim, 0)


def summed_on_arrival(array, axis, dim):
    peers = lax.axis_size(axis)
    tiles = lax.all_to_all(cut_along(array, dim, peers), axis, 0, 0, tiled=True)
    return jnp.sum(tiles.astype(jnp.float32), axis=0)


def sent_together(arrays, axis, dim, along):
    widths = [a.shape[along] for a in arrays]
    both = jnp.concatenate(arrays, axis=along)
    result = summed_on_arrival(both, axis, dim)
    return tuple(jnp.split(result, [sum(widths[:k]) for k in range(1, len(widths))], axis=along))


def cell_math(conv, state_prev, vector, cell_mask):
    width = state_prev.shape[-1]
    pre_act = conv + vector[: 4 * width]
    gate_in = jax.nn.sigmoid(pre_act[..., :width] + vector[4 * width : 5 * width] * state_prev)
    gate_keep = jax.nn.sigmoid(
        pre_act[..., width : 2 * width] + vector[5 * width : 6 * width] * state_prev
    )
    candidate = jnp.tanh(pre_act[..., 2 * width : 3 * width])
    state_new = (gate_keep * state_prev + gate_in * candidate) * cell_mask
    gate_out = jax.nn.sigmoid(pre_act[..., 3 * width :] + vector[6 * width :] * state_new)
    return (gate_out * jnp.tanh(state_new), state_new)


def pad_columns(field):
    return jnp.pad(field, ((0, 0), (1, 1), (0, 0)))


def forward_taps(padded, row_count, col_count):
    pieces = [
        padded[tap_row : tap_row + row_count, tap_col : tap_col + col_count]
        for tap_row in range(3)
        for tap_col in range(3)
    ]
    return jnp.concatenate(pieces, axis=-1).reshape(row_count * col_count, -1)


def backward_taps(padded, row_count, col_count):
    pieces = [
        padded[2 - tap_row : 2 - tap_row + row_count, 2 - tap_col : 2 - tap_col + col_count]
        for tap_row in range(3)
        for tap_col in range(3)
    ]
    return jnp.stack(pieces, axis=2).reshape(row_count * col_count, 9, -1)


def apply_weights(patches, weight):
    return lax.dot_general(
        patches, weight, (((1,), (1,)), ((), ())), preferred_element_type=jnp.float32
    )


def weight_grad(gate_grad, patches):
    return lax.dot_general(
        gate_grad, patches, (((0,), (0,)), ((), ())), preferred_element_type=jnp.float32
    )


def spread_back(grad_taps, weight):
    taps_weight = weight.reshape(weight.shape[0], 9, -1)
    return jnp.einsum("nkg,gkc->nc", grad_taps, taps_weight, preferred_element_type=jnp.float32)


def extend_rows(field, axis):
    extent = field.shape[axis]
    last_row = lax.slice_in_dim(field, extent - 1, extent, axis=axis)
    first_row = lax.slice_in_dim(field, 0, 1, axis=axis)
    above = from_behind(last_row, "band", 1)
    below = from_behind(first_row, "band", -1)
    return jnp.concatenate([above, field, below], axis=axis)


def extend_grads(field):
    above = from_behind(field[-1:], "band", 1)
    below = from_behind(field[:1], "band", -1)
    return jnp.concatenate([above, field, below], axis=0)


def adam_update(weight, moment_one, moment_two, grad, rate):
    first_new = beta_first * moment_one + (1.0 - beta_first) * grad
    second_new = beta_second * moment_two + (1.0 - beta_second) * grad * grad
    scale_one = 1.0 - beta_first**STEP
    scale_two = 1.0 - beta_second**STEP
    direction = first_new / scale_one / (jnp.sqrt(second_new / scale_two) + adam_epsilon)
    fresh = weight - rate * (direction + weight_decay * weight)
    return (fresh, first_new, second_new, fresh.astype(jnp.bfloat16))


def local(
    frames,
    grid_size,
    out_grad,
    enc_hidden,
    enc_hidden_m,
    enc_hidden_v,
    fore_hidden,
    fore_hidden_m,
    fore_hidden_v,
    enc_input,
    enc_input_m,
    enc_input_v,
    cell_vectors,
    vectors_m,
    vectors_v,
):
    device_place = lax.axis_index("band")
    row_count = frames.shape[2]
    width = HID
    gate_count = 4 * width
    col_count = out_grad.shape[3] // width
    channels = frames.shape[3] // col_count
    row_start = device_place * row_count
    cell_total = row_count * col_count
    row_ids = row_start + lax.iota(jnp.int32, row_count)
    col_ids = lax.iota(jnp.int32, col_count)
    inside = (row_ids[:, None] < grid_size[0, 0]) & (col_ids[None, :] < grid_size[0, 1])
    cell_mask = inside.astype(jnp.float32).reshape(cell_total, 1)
    frame_cells = frames[0].reshape(FRAMES_IN, row_count, col_count, channels)
    inputs_masked = jnp.where(inside[None, :, :, None], frame_cells, jnp.zeros_like(frame_cells))
    inputs_rimmed = extend_rows(inputs_masked, 1)
    copies = (
        enc_hidden.astype(jnp.bfloat16),
        fore_hidden.astype(jnp.bfloat16),
        enc_input.astype(jnp.bfloat16),
        cell_vectors.astype(jnp.bfloat16),
    )
    w_enc, w_fore, w_input, vector_all = (
        lax.all_gather(copies[0], "band", axis=0, tiled=True),
        lax.all_gather(copies[1], "band", axis=0, tiled=True),
        lax.all_gather(copies[2], "band", axis=0, tiled=True),
        lax.all_gather(copies[3], "band", axis=0, tiled=True),
    )
    vector_enc = vector_all[: 7 * width].astype(jnp.float32)
    vector_fore = vector_all[7 * width :].astype(jnp.float32)

    def enc_forward(carry, input_rim):
        hidden, state = carry
        hidden_pad = pad_columns(extend_rows(hidden, 0))
        input_pad = pad_columns(input_rim)
        conv = apply_weights(forward_taps(hidden_pad, row_count, col_count), w_enc) + apply_weights(
            forward_taps(input_pad, row_count, col_count), w_input
        )
        out_hidden, out_state = cell_math(conv, state, vector_enc, cell_mask)
        new_hidden = out_hidden.astype(jnp.bfloat16).reshape(row_count, col_count, width)
        return ((new_hidden, out_state), (hidden_pad, state))

    zero_hidden = jnp.zeros((row_count, col_count, width), jnp.bfloat16)
    zero_state = jnp.zeros((cell_total, width), jnp.float32)
    (start_hidden, start_state), (enc_pads, enc_states) = lax.scan(
        enc_forward, (zero_hidden, zero_state), inputs_rimmed
    )

    def fore_forward(carry, unused):
        hidden, state = carry
        hidden_pad = pad_columns(extend_rows(hidden, 0))
        conv = apply_weights(forward_taps(hidden_pad, row_count, col_count), w_fore)
        out_hidden, out_state = cell_math(conv, state, vector_fore, cell_mask)
        new_hidden = out_hidden.astype(jnp.bfloat16).reshape(row_count, col_count, width)
        return ((new_hidden, out_state), (hidden_pad, state, new_hidden))

    _, (fore_pads, fore_states, fore_outputs) = lax.scan(
        fore_forward, (start_hidden, start_state), None, length=FRAMES_OUT
    )
    out_cot = out_grad[0].reshape(FRAMES_OUT, cell_total, width)

    def fore_backward(carry, inputs):
        hidden_grad, state_grad, weight_sum, vector_sum = carry
        hidden_pad, state_prev, cot_step = inputs
        total_grad = hidden_grad + cot_step.astype(jnp.float32)
        patches = forward_taps(hidden_pad, row_count, col_count)
        conv = apply_weights(patches, w_fore)
        _, pull = jax.vjp(
            lambda conv_in, state_in, vector_in: cell_math(conv_in, state_in, vector_in, cell_mask),
            conv,
            state_prev,
            vector_fore,
        )
        conv_grad, prev_grad, vector_grad = pull((total_grad, state_grad))
        gate_grad = conv_grad.astype(jnp.bfloat16)
        grad_pad = pad_columns(extend_grads(gate_grad.reshape(row_count, col_count, gate_count)))
        back_hidden = spread_back(backward_taps(grad_pad, row_count, col_count), w_fore)
        step_weight = weight_grad(gate_grad, patches)
        return ((back_hidden, prev_grad, weight_sum + step_weight, vector_sum + vector_grad), None)

    fore_init = (
        jnp.zeros((cell_total, width), jnp.float32),
        jnp.zeros((cell_total, width), jnp.float32),
        jnp.zeros((gate_count, 9 * width), jnp.float32),
        jnp.zeros((7 * width,), jnp.float32),
    )
    (enc_hidden_grad, enc_state_grad, fore_weight_grad, fore_vector_grad), _ = lax.scan(
        fore_backward, fore_init, (fore_pads, fore_states, out_cot), reverse=True
    )

    def enc_backward(carry, inputs):
        hidden_grad, state_grad, weight_sum, input_sum, vector_sum = carry
        hidden_pad, input_rim, state_prev = inputs
        input_pad = pad_columns(input_rim)
        hidden_patches = forward_taps(hidden_pad, row_count, col_count)
        input_patches = forward_taps(input_pad, row_count, col_count)
        conv = apply_weights(hidden_patches, w_enc) + apply_weights(input_patches, w_input)
        _, pull = jax.vjp(
            lambda conv_in, state_in, vector_in: cell_math(conv_in, state_in, vector_in, cell_mask),
            conv,
            state_prev,
            vector_enc,
        )
        conv_grad, prev_grad, vector_grad = pull((hidden_grad, state_grad))
        gate_grad = conv_grad.astype(jnp.bfloat16)
        grad_pad = pad_columns(extend_grads(gate_grad.reshape(row_count, col_count, gate_count)))
        grad_taps = backward_taps(grad_pad, row_count, col_count)
        back_hidden = spread_back(grad_taps, w_enc)
        back_input = spread_back(grad_taps, w_input) * cell_mask
        step_weight = weight_grad(gate_grad, hidden_patches)
        step_input = weight_grad(gate_grad, input_patches)
        return (
            (
                back_hidden,
                prev_grad,
                weight_sum + step_weight,
                input_sum + step_input,
                vector_sum + vector_grad,
            ),
            back_input,
        )

    enc_init = (
        enc_hidden_grad,
        enc_state_grad,
        jnp.zeros((gate_count, 9 * width), jnp.float32),
        jnp.zeros((gate_count, 9 * channels), jnp.float32),
        jnp.zeros((7 * width,), jnp.float32),
    )
    (_, _, enc_weight_grad, input_weight_grad, enc_vector_grad), input_grads = lax.scan(
        enc_backward, enc_init, (enc_pads, inputs_rimmed, enc_states), reverse=True
    )
    hidden_block = fore_outputs.reshape(FRAMES_OUT, row_count, col_count * width)
    input_block = input_grads.reshape(FRAMES_IN, row_count, col_count * channels)
    vector_grad_all = jnp.concatenate([enc_vector_grad, fore_vector_grad])
    shares = (
        *sent_together(
            (
                enc_weight_grad.astype(jnp.bfloat16),
                fore_weight_grad.astype(jnp.bfloat16),
                input_weight_grad.astype(jnp.bfloat16),
            ),
            "band",
            0,
            1,
        ),
        summed_on_arrival(vector_grad_all.astype(jnp.bfloat16), "band", 0),
    )
    enc_share, fore_share, input_share, vector_share = (
        lax.psum(shares[0].astype(jnp.bfloat16), "grp").astype(jnp.float32),
        lax.psum(shares[1].astype(jnp.bfloat16), "grp").astype(jnp.float32),
        lax.psum(shares[2].astype(jnp.bfloat16), "grp").astype(jnp.float32),
        lax.psum(shares[3].astype(jnp.bfloat16), "grp").astype(jnp.float32),
    )
    enc_new, enc_one, enc_two, enc_copy = adam_update(
        enc_hidden, enc_hidden_m, enc_hidden_v, enc_share, matrix_rate
    )
    fore_new, fore_one, fore_two, fore_copy = adam_update(
        fore_hidden, fore_hidden_m, fore_hidden_v, fore_share, matrix_rate
    )
    input_new, input_one, input_two, input_copy = adam_update(
        enc_input, enc_input_m, enc_input_v, input_share, matrix_rate
    )
    vector_new, vector_one, vector_two, vector_copy = adam_update(
        cell_vectors, vectors_m, vectors_v, vector_share, vector_rate
    )
    return (
        hidden_block[None],
        input_block[None],
        enc_new,
        enc_one,
        enc_two,
        enc_copy,
        fore_new,
        fore_one,
        fore_two,
        fore_copy,
        input_new,
        input_one,
        input_two,
        input_copy,
        vector_new,
        vector_one,
        vector_two,
        vector_copy,
    )


def solution(mesh):
    return jax.shard_map(
        local,
        mesh=mesh,
        in_specs=(
            P("grp", None, "band", None),
            P("grp", None),
            P("grp", None, "band", None),
            P("band", None),
            P("band", None),
            P("band", None),
            P("band", None),
            P("band", None),
            P("band", None),
            P("band", None),
            P("band", None),
            P("band", None),
            P("band"),
            P("band"),
            P("band"),
        ),
        out_specs=(
            P("grp", None, "band", None),
            P("grp", None, "band", None),
            P("band", None),
            P("band", None),
            P("band", None),
            P("band", None),
            P("band", None),
            P("band", None),
            P("band", None),
            P("band", None),
            P("band", None),
            P("band", None),
            P("band", None),
            P("band", None),
            P("band"),
            P("band"),
            P("band"),
            P("band"),
        ),
        check_vma=False,
    )
```

profile of v0, /device:TPU:0, one launch (start us, length us, event | category | flops | bytes accessed | tf_op | source)
XLA Modules:
  0.0 833.1 jit_solution(7778554112628853116)
XLA Ops:
  21.1 19.1 %all-reduce.22 = bf16[1792]{0:T(1024)(128)(2,1)S(1)} all-reduce(bf16[1792]{0:T(1024)(128)(2,1)S(1)} %dynamic-update-slice), channel_id=1, replica_groups=mesh['grp'=4,'band'=8] {'band'}, use_global_device_ids=true, to_apply=%add.22 | all-reduce | flops 1792 | bytes 7168
  40.1 15.1 %all_gather.13 = bf16[512,144]{1,0:T(8,128)(2,1)S(1)} all-gather(bf16[64,144]{1,0:T(8,128)(2,1)S(1)} %convert_element_type.141), channel_id=1, replica_groups=mesh['grp'=4,'band'=8] {'band'}, dimensions={0}, use_global_device_ids=true | all-gather | bytes 165888 | tf_op jit(solution)/shard_map/all_gather | solution.py:163
  64.1 71.5 %while.87 = (s32[]{:T(128)}, bf16[2,128,128]{2,1,0:T(8,128)(2,1)S(1)}, f32[256,128]{1,0:T(8,128)S(1)}, bf16[5,4,130,128]{3,2,1,0:T(8,128)(2,1)}, f32[5,256,128]{...) while((s32[]{:T(128)}, ...), condition=%wide.region_1.2_spmd.clone, body=%wide.region_0.1_spmd.clone.sunk | while | flops 342614528 | bytes 7457754 | solution.py:182
  136.3 161.4 %while.86 = (s32[]{:T(128)}, bf16[2,128,128]{2,1,0:T(8,128)(2,1)S(1)}, f32[256,128]{1,0:T(8,128)S(1)}, bf16[15,4,130,128]{3,2,1,0:T(8,128)(2,1)}, f32[15,256,128...) while((s32[]{:T(128)}, ...), condition=%wide.region_3.4_spmd.clone, body=%wide.region_2.3_spmd.clone.sunk | while | flops 304669184 | bytes 5725011 | solution.py:194
  158.8 4.4 collective-permute-start.1
  169.6 4.4 collective-permute-start.1
  180.4 4.4 collective-permute-start.1
  191.2 4.4 collective-permute-start.1
  202.0 4.4 collective-permute-start.1
  234.3 4.5 collective-permute-start.1
  245.1 4.4 collective-permute-start.1
  255.9 4.4 collective-permute-start.1
  266.6 4.4 collective-permute-start.1
  277.4 4.4 collective-permute-start.1
  288.2 4.4 collective-permute-start.1
  297.7 300.0 %while.88 = (s32[]{:T(128)}, f32[256,128]{1,0:T(8,128)S(1)}, f32[256,128]{1,0:T(8,128)S(1)}, f32[512,1152]{1,0:T(8,128)}, f32[896]{0:T(1024)S(1)}, /*index=5*/bf...) while((s32[]{:T(128)}, f32[256,128]{1,0:T(8,128)S(1)}, ...), condition=%wide.region_9.10_spmd.clone, body=%wide.region_4.9_spmd.clone.sunk | while | flops 913559552 | bytes 30975444 | solution.py:224
  305.2 5.1 collective-permute-start.5
  324.4 4.5 collective-permute-start.5
  344.6 4.6 collective-permute-start.5
  597.8 92.1 %while.89 = (s32[]{:T(128)}, f32[256,128]{1,0:T(8,128)S(1)}, f32[256,128]{1,0:T(8,128)S(1)}, f32[512,1152]{1,0:T(8,128)}, f32[512,144]{0,1:T(8,128)}, /*index=5*...) while((s32[]{:T(128)}, f32[256,128]{1,0:T(8,128)S(1)}, ...), condition=%wide.region_15.16_spmd.clone, body=%wide.region_10.15_spmd.clone.sunk | while | flops 1026924544 | bytes 36645388 | solution.py:267
  700.2 4.9 all-to-all-start
  709.8 55.7 %all-to-all-done = bf16[8,64,2448]{2,1,0:T(8,128)(2,1)S(1)} async-done(((bf16[8,64,2448]{2,1,0:T(8,128)(2,1)}), bf16[8,64,2448]{2,1,0:T(8,128)(2,1)S(1)}, u32[]{:S(2)}, u32[]{:S(2)}) %all-to-all-start) | async-done | bytes 2506784 | tf_op jit(solution)/shard_map/all_to_all | solution.py:34
  766.5 16.7 %all-reduce.23 = (bf16[64,144]{1,0:T(8,128)(2,1)S(1)}, bf16[224]{0:T(256)(128)(2,1)S(1)}) all-reduce(bf16[64,144]{1,0:T(8,128)(2,1)S(1)} %split.17, bf16[224]{0:T(256)(128)(2,1)S(1)} %reduce_sum.174), channel_id=1, replica_groups=mesh['grp'=4,'band'=8] {'grp'}, use_global_device_ids=true, to_apply=%region_19.20 | all-reduce | flops 9440 | bytes 37760 | tf_op jit(solution)/shard_map/psum | solution.py:289
  785.5 38.3 %all-reduce.27.cloned.1.call-done = (bf16[64,1152]{1,0:T(8,128)(2,1)}, bf16[64,1152]{1,0:T(8,128)(2,1)}) async-done(((bf16[64,1152]{1,0:T(8,128)(2,1)}, bf16[64,1152]{1,0:T(8,128)(2,1)}), (bf16[64,1152]{1,0:T(8,128)(2,1)}, bf16[64,1152]{1,0:T(8,128)(2,1)})) %all-reduce.27.cloned.1.call-update) | async-done | bytes 294928 | tf_op jit(solution)/shard_map/psum | solution.py:287
  (1573 shorter events, 598.8 us)
Async XLA Ops:
  7.2 50.4 %all-gather.5.cloned.1.call-start = ((), (), s32[]{:S(2)}) async-start(), calls=%async_computation.3 | async-start | bytes 1327104 | tf_op jit(solution)/shard_map/all_gather | solution.py:162
  9.0 53.5 %all-gather.3.cloned.1.call-start = ((), (), s32[]{:S(2)}) async-start(), calls=%async_computation.2 | async-start | bytes 1327104 | tf_op jit(solution)/shard_map/all_gather | solution.py:161
  15.8 41.4 %collective-permute-start.8 = (bf16[5,1,128,16]{3,2,1,0:T(8,128)(2,1)S(1)}, bf16[5,1,128,16]{3,2,1,0:T(8,128)(2,1)S(1)}, u32[]{:S(2)}, u32[]{:S(2)}) collective-permute-start(bf16[5,1,128,16]{3,2,1,0:T(8,128)(2,1)S(1)} %get-tuple-element.1223), channel_id=1, source_target_pairs={{0,1},{1,2},{2,3},{3,4},{4,5},{5,6},{6,7},{8,9},{9,10},{10,11},{11... | collective-permute-start | bytes 61448 | tf_op jit(solution)/shard_map/ppermute | solution.py:23
  18.2 39.2 %collective-permute-start.9 = (bf16[5,1,128,16]{3,2,1,0:T(8,128)(2,1)S(1)}, bf16[5,1,128,16]{3,2,1,0:T(8,128)(2,1)S(1)}, u32[]{:S(2)}, u32[]{:S(2)}) collective-permute-start(bf16[5,1,128,16]{3,2,1,0:T(8,128)(2,1)S(1)} %get-tuple-element.1224), channel_id=1, source_target_pairs={{1,0},{2,1},{3,2},{4,3},{5,4},{6,5},{7,6},{9,8},{10,9},{11,10},{12... | collective-permute-start | bytes 61448 | tf_op jit(solution)/shard_map/ppermute | solution.py:23
  78.1 10.0 %collective-permute-start.2 = (bf16[1,128,128]{2,1,0:T(8,128)(2,1)}, bf16[1,128,128]{2,1,0:T(8,128)(2,1)S(1)}, u32[]{:S(2)}, u32[]{:S(2)}) collective-permute-start(bf16[1,128,128]{2,1,0:T(8,128)(2,1)} %get-tuple-element.1600), channel_id=1, source_target_pairs={{1,0},{2,1},{3,2},{4,3},{5,4},{6,5},{7,6},{9,8},{10,9},{11,10},{12... | collective-permute-start | bytes 98312 | tf_op jit(solution)/shard_map/while/body/eval_jaxpr/ppermute | solution.py:23
  92.5 10.3 %collective-permute-start.2 = (bf16[1,128,128]{2,1,0:T(8,128)(2,1)}, bf16[1,128,128]{2,1,0:T(8,128)(2,1)S(1)}, u32[]{:S(2)}, u32[]{:S(2)}) collective-permute-start(bf16[1,128,128]{2,1,0:T(8,128)(2,1)} %get-tuple-element.1600), channel_id=1, source_target_pairs={{1,0},{2,1},{3,2},{4,3},{5,4},{6,5},{7,6},{9,8},{10,9},{11,10},{12... | collective-permute-start | bytes 98312 | tf_op jit(solution)/shard_map/while/body/eval_jaxpr/ppermute | solution.py:23
  107.1 10.3 %collective-permute-start.2 = (bf16[1,128,128]{2,1,0:T(8,128)(2,1)}, bf16[1,128,128]{2,1,0:T(8,128)(2,1)S(1)}, u32[]{:S(2)}, u32[]{:S(2)}) collective-permute-start(bf16[1,128,128]{2,1,0:T(8,128)(2,1)} %get-tuple-element.1600), channel_id=1, source_target_pairs={{1,0},{2,1},{3,2},{4,3},{5,4},{6,5},{7,6},{9,8},{10,9},{11,10},{12... | collective-permute-start | bytes 98312 | tf_op jit(solution)/shard_map/while/body/eval_jaxpr/ppermute | solution.py:23
  121.7 10.3 %collective-permute-start.2 = (bf16[1,128,128]{2,1,0:T(8,128)(2,1)}, bf16[1,128,128]{2,1,0:T(8,128)(2,1)S(1)}, u32[]{:S(2)}, u32[]{:S(2)}) collective-permute-start(bf16[1,128,128]{2,1,0:T(8,128)(2,1)} %get-tuple-element.1600), channel_id=1, source_target_pairs={{1,0},{2,1},{3,2},{4,3},{5,4},{6,5},{7,6},{9,8},{10,9},{11,10},{12... | collective-permute-start | bytes 98312 | tf_op jit(solution)/shard_map/while/body/eval_jaxpr/ppermute | solution.py:23
  323.1 9.4 %collective-permute-start.4 = (bf16[1,128,512]{2,1,0:T(8,128)(2,1)}, bf16[1,128,512]{2,1,0:T(8,128)(2,1)S(1)}, u32[]{:S(2)}, u32[]{:S(2)}) collective-permute-start(bf16[1,128,512]{2,1,0:T(8,128)(2,1)} %get-tuple-element.1631), channel_id=1, source_target_pairs={{1,0},{2,1},{3,2},{4,3},{5,4},{6,5},{7,6},{9,8},{10,9},{11,10},{12... | collective-permute-start | bytes 393224 | tf_op jit(solution)/shard_map/while/body/eval_jaxpr/ppermute | solution.py:23
  343.3 9.5 %collective-permute-start.4 = (bf16[1,128,512]{2,1,0:T(8,128)(2,1)}, bf16[1,128,512]{2,1,0:T(8,128)(2,1)S(1)}, u32[]{:S(2)}, u32[]{:S(2)}) collective-permute-start(bf16[1,128,512]{2,1,0:T(8,128)(2,1)} %get-tuple-element.1631), channel_id=1, source_target_pairs={{1,0},{2,1},{3,2},{4,3},{5,4},{6,5},{7,6},{9,8},{10,9},{11,10},{12... | collective-permute-start | bytes 393224 | tf_op jit(solution)/shard_map/while/body/eval_jaxpr/ppermute | solution.py:23
  363.6 9.2 %collective-permute-start.4 = (bf16[1,128,512]{2,1,0:T(8,128)(2,1)}, bf16[1,128,512]{2,1,0:T(8,128)(2,1)S(1)}, u32[]{:S(2)}, u32[]{:S(2)}) collective-permute-start(bf16[1,128,512]{2,1,0:T(8,128)(2,1)} %get-tuple-element.1631), channel_id=1, source_target_pairs={{1,0},{2,1},{3,2},{4,3},{5,4},{6,5},{7,6},{9,8},{10,9},{11,10},{12... | collective-permute-start | bytes 393224 | tf_op jit(solution)/shard_map/while/body/eval_jaxpr/ppermute | solution.py:23
  383.6 9.2 %collective-permute-start.4 = (bf16[1,128,512]{2,1,0:T(8,128)(2,1)}, bf16[1,128,512]{2,1,0:T(8,128)(2,1)S(1)}, u32[]{:S(2)}, u32[]{:S(2)}) collective-permute-start(bf16[1,128,512]{2,1,0:T(8,128)(2,1)} %get-tuple-element.1631), channel_id=1, source_target_pairs={{1,0},{2,1},{3,2},{4,3},{5,4},{6,5},{7,6},{9,8},{10,9},{11,10},{12... | collective-permute-start | bytes 393224 | tf_op jit(solution)/shard_map/while/body/eval_jaxpr/ppermute | solution.py:23
  403.7 9.2 %collective-permute-start.4 = (bf16[1,128,512]{2,1,0:T(8,128)(2,1)}, bf16[1,128,512]{2,1,0:T(8,128)(2,1)S(1)}, u32[]{:S(2)}, u32[]{:S(2)}) collective-permute-start(bf16[1,128,512]{2,1,0:T(8,128)(2,1)} %get-tuple-element.1631), channel_id=1, source_target_pairs={{1,0},{2,1},{3,2},{4,3},{5,4},{6,5},{7,6},{9,8},{10,9},{11,10},{12... | collective-permute-start | bytes 393224 | tf_op jit(solution)/shard_map/while/body/eval_jaxpr/ppermute | solution.py:23
  443.7 9.2 %collective-permute-start.4 = (bf16[1,128,512]{2,1,0:T(8,128)(2,1)}, bf16[1,128,512]{2,1,0:T(8,128)(2,1)S(1)}, u32[]{:S(2)}, u32[]{:S(2)}) collective-permute-start(bf16[1,128,512]{2,1,0:T(8,128)(2,1)} %get-tuple-element.1631), channel_id=1, source_target_pairs={{1,0},{2,1},{3,2},{4,3},{5,4},{6,5},{7,6},{9,8},{10,9},{11,10},{12... | collective-permute-start | bytes 393224 | tf_op jit(solution)/shard_map/while/body/eval_jaxpr/ppermute | solution.py:23
  463.7 9.2 %collective-permute-start.4 = (bf16[1,128,512]{2,1,0:T(8,128)(2,1)}, bf16[1,128,512]{2,1,0:T(8,128)(2,1)S(1)}, u32[]{:S(2)}, u32[]{:S(2)}) collective-permute-start(bf16[1,128,512]{2,1,0:T(8,128)(2,1)} %get-tuple-element.1631), channel_id=1, source_target_pairs={{1,0},{2,1},{3,2},{4,3},{5,4},{6,5},{7,6},{9,8},{10,9},{11,10},{12... | collective-permute-start | bytes 393224 | tf_op jit(solution)/shard_map/while/body/eval_jaxpr/ppermute | solution.py:23
  523.8 9.2 %collective-permute-start.4 = (bf16[1,128,512]{2,1,0:T(8,128)(2,1)}, bf16[1,128,512]{2,1,0:T(8,128)(2,1)S(1)}, u32[]{:S(2)}, u32[]{:S(2)}) collective-permute-start(bf16[1,128,512]{2,1,0:T(8,128)(2,1)} %get-tuple-element.1631), channel_id=1, source_target_pairs={{1,0},{2,1},{3,2},{4,3},{5,4},{6,5},{7,6},{9,8},{10,9},{11,10},{12... | collective-permute-start | bytes 393224 | tf_op jit(solution)/shard_map/while/body/eval_jaxpr/ppermute | solution.py:23
  583.9 9.2 %collective-permute-start.4 = (bf16[1,128,512]{2,1,0:T(8,128)(2,1)}, bf16[1,128,512]{2,1,0:T(8,128)(2,1)S(1)}, u32[]{:S(2)}, u32[]{:S(2)}) collective-permute-start(bf16[1,128,512]{2,1,0:T(8,128)(2,1)} %get-tuple-element.1631), channel_id=1, source_target_pairs={{1,0},{2,1},{3,2},{4,3},{5,4},{6,5},{7,6},{9,8},{10,9},{11,10},{12... | collective-permute-start | bytes 393224 | tf_op jit(solution)/shard_map/while/body/eval_jaxpr/ppermute | solution.py:23
  621.2 9.6 %collective-permute-start.6 = (bf16[1,128,512]{2,1,0:T(8,128)(2,1)S(1)}, bf16[1,128,512]{2,1,0:T(8,128)(2,1)S(1)}, u32[]{:S(2)}, u32[]{:S(2)}) collective-permute-start(bf16[1,128,512]{2,1,0:T(8,128)(2,1)S(1)} %get-tuple-element.1682), channel_id=1, source_target_pairs={{1,0},{2,1},{3,2},{4,3},{5,4},{6,5},{7,6},{9,8},{10,9},{11,10},{12... | collective-permute-start | bytes 393224 | tf_op jit(solution)/shard_map/while/body/eval_jaxpr/ppermute | solution.py:23
  640.1 9.6 %collective-permute-start.6 = (bf16[1,128,512]{2,1,0:T(8,128)(2,1)S(1)}, bf16[1,128,512]{2,1,0:T(8,128)(2,1)S(1)}, u32[]{:S(2)}, u32[]{:S(2)}) collective-permute-start(bf16[1,128,512]{2,1,0:T(8,128)(2,1)S(1)} %get-tuple-element.1682), channel_id=1, source_target_pairs={{1,0},{2,1},{3,2},{4,3},{5,4},{6,5},{7,6},{9,8},{10,9},{11,10},{12... | collective-permute-start | bytes 393224 | tf_op jit(solution)/shard_map/while/body/eval_jaxpr/ppermute | solution.py:23
  659.0 9.6 %collective-permute-start.6 = (bf16[1,128,512]{2,1,0:T(8,128)(2,1)S(1)}, bf16[1,128,512]{2,1,0:T(8,128)(2,1)S(1)}, u32[]{:S(2)}, u32[]{:S(2)}) collective-permute-start(bf16[1,128,512]{2,1,0:T(8,128)(2,1)S(1)} %get-tuple-element.1682), channel_id=1, source_target_pairs={{1,0},{2,1},{3,2},{4,3},{5,4},{6,5},{7,6},{9,8},{10,9},{11,10},{12... | collective-permute-start | bytes 393224 | tf_op jit(solution)/shard_map/while/body/eval_jaxpr/ppermute | solution.py:23
  677.9 9.6 %collective-permute-start.6 = (bf16[1,128,512]{2,1,0:T(8,128)(2,1)S(1)}, bf16[1,128,512]{2,1,0:T(8,128)(2,1)S(1)}, u32[]{:S(2)}, u32[]{:S(2)}) collective-permute-start(bf16[1,128,512]{2,1,0:T(8,128)(2,1)S(1)} %get-tuple-element.1682), channel_id=1, source_target_pairs={{1,0},{2,1},{3,2},{4,3},{5,4},{6,5},{7,6},{9,8},{10,9},{11,10},{12... | collective-permute-start | bytes 393224 | tf_op jit(solution)/shard_map/while/body/eval_jaxpr/ppermute | solution.py:23
  690.7 9.4 %all-to-all-start.1 = ((bf16[8,1,224]{2,1,0:T(2,128)(2,1)}), bf16[8,1,224]{2,1,0:T(2,128)(2,1)S(1)}, u32[]{:S(2)}, u32[]{:S(2)}) async-start(bf16[8,1,224]{2,1,0:T(2,128)(2,1)} %copy.63), calls=%async_computation.1 | async-start | bytes 16384 | tf_op jit(solution)/shard_map/all_to_all | solution.py:34
  700.2 65.2 %all-to-all-start = ((bf16[8,64,2448]{2,1,0:T(8,128)(2,1)}), bf16[8,64,2448]{2,1,0:T(8,128)(2,1)S(1)}, u32[]{:S(2)}, u32[]{:S(2)}) async-start(bf16[8,64,2448]{2,1,0:T(8,128)(2,1)} %bitcast.3), calls=%async_computation | async-start | bytes 5242880 | tf_op jit(solution)/shard_map/all_to_all | solution.py:34
  705.1 118.7 %all-reduce.27.cloned.1.call-start = ((), (), s32[]{:S(2)}) async-start(), calls=%async_computation.4 | async-start | bytes 589824 | tf_op jit(solution)/shard_map/psum | solution.py:287
  (142 other events, 1549.0 us)
Sparse Core Ops, SparseCore 0:
  10.3 27.3 all-gather.4
  39.9 22.5 all-gather.2
  783.4 40.3 all-reduce.26
where the time goes:
time: 841 us; the launch traced here: 833 us
  starting transfers between devices  236 us (28%)
  other arithmetic  161 us (19%)
  matrix products  143 us (17%)
  local copies, waits for them, and re-layouts  122 us (15%)
  waiting for transfers between devices  97.8 us (12%)
  blocking collectives  50.8 us (6%)
  between operations  14.9 us (2%)
    ppermute x82, starting transfers between devices, from_behind(): lax.ppermute(value, axis, [(source, source + steps) for source in range(f...  227 us
    dot_general x25, matrix products, weight_grad(): lax.dot_general(gate_grad, patches, (((0,), (0,)), ((), ())), preferred_e...  70.9 us
    all_to_all x2, waiting for transfers between devices, summed_on_arrival(): tiles = lax.all_to_all(cut_along(array, dim, peers), axis, 0, 0, tiled=True)  55.8 us
    dot_general x50, matrix products, apply_weights(): lax.dot_general(patches, weight, (((1,), (1,)), ((), ())), preferred_elem...  53.8 us
    psum x1, waiting for transfers between devices, local(): lax.psum(shares[0].astype(jnp.bfloat16), 'grp').astype(jnp.float32)  38.3 us
    while x650, local copies, waits for them, and re-layouts  37.3 us
    mul x40, other arithmetic, cell_math(): state_new = (gate_keep * state_prev + gate_in * candidate) * cell_mask  31.9 us
    concatenate x40, other arithmetic, extend_grads(): return jnp.concatenate([above, field, below], axis=0)  30.9 us
  transfers between devices with their start and end apart: 87, of which 4 were waited for; matrix products, arithmetic and copies ran while one was open for 16% of the time, Pallas kernels for 0%

commit v1 on v0

--- a/solution.py
+++ b/solution.py
@@ -1,6 +1,12 @@
+import functools
+
 import jax
 import jax.numpy as jnp
+import numpy as np
 from jax import lax
+from jax.experimental import pallas as pl
+from jax.experimental.pallas import tpu as pltpu
+from jax.sharding import Mesh
 from jax.sharding import PartitionSpec as P
 
 HID = 128
@@ -119,7 +125,7 @@
     return (fresh, first_new, second_new, fresh.astype(jnp.bfloat16))
 
 
-def local(
+def by_rows(
     frames,
     grid_size,
     out_grad,
@@ -323,46 +329,1215 @@
     )
 
 
+f32 = jnp.float32
+bf16 = jnp.bfloat16
+
+GRID_ROWS = 16
+STRIP = 16
+FRAME_COLS = 80
+OWN = 32
+REACH = 10
+REACH_MID = 5
+KEPT = STRIP + 2 * REACH
+ENC_REACH = 6
+ENC_KEPT = STRIP + 2 * ENC_REACH
+ENC_COLS = (3, 77)
+PIECE_ROWS = 80
+PIECE_LANES = 1408
+ENC_RUNS = ((1, 28, 24), (3, 26, 23))
+FORE_RUNS = ((0, 24, 22), (2, 22, 20), (5, 19, 18), (7, 17, 17), (10, 14, 22), (12, 12, 20))
+LATE_RUNS = ((0, 10, 18), (2, 8, 16), (5, 5, 13), (7, 3, 11))
+EARLY_RUNS = ((0, 10, 18), (2, 8, 16))
+ENC_BACK_RUNS = ((0, 5, 13), (2, 3, 11))
+MIB = 1024 * 1024
+LARGE, LONG, MIDDLE, SMALL = 60, 56, 52, 24
+
+
+def cells(first, count):
+    return pl.ds(pl.multiple_of(first * GRID_ROWS, GRID_ROWS), count * GRID_ROWS)
+
+
+def gate(value):
+    return 0.5 * jnp.tanh(0.5 * value) + 0.5
+
+
+def row_moves(value):
+    total = value.shape[0]
+    row = lax.broadcasted_iota(jnp.int32, value.shape, 0) & (GRID_ROWS - 1)
+    above = jnp.where(row == 0, 0.0, pltpu.roll(value, 1, 0))
+    below = jnp.where(row == GRID_ROWS - 1, 0.0, pltpu.roll(value, total - 1, 0))
+    return above, below
+
+
+def own_column():
+    return STRIP * (2 * lax.axis_index("z") + lax.axis_index("core"))
+
+
+def runs_of(runs, steps, step_id, run):
+    for k, (first, halo, piece) in enumerate(runs):
+        end = runs[k + 1][0] if k + 1 < len(runs) else steps
+        pl.when((step_id >= first) & (step_id < end))(functools.partial(run, first, halo, piece))
+
+
+def fill_mask(lim_ref, mask_ref, first_col):
+    shape = mask_ref.shape
+    place = lax.broadcasted_iota(jnp.int32, shape, 0)
+    row = place & (GRID_ROWS - 1)
+    col = (place >> 4) + (own_column() + first_col)
+    inside = (row < lim_ref[0, 0]) & (col >= 0) & (col < lim_ref[0, 1])
+    mask_ref[...] = jnp.where(inside, 1.0, 0.0)
+
+
+def tile_rows(first, count):
+    return slice(first * GRID_ROWS, (first + count) * GRID_ROWS)
+
+
+def cuts(first, last, size, inner=()):
+    edges = sorted({first, last, *[edge for edge in inner if first < edge < last]})
+    pieces = []
+    for lo, hi in zip(edges[:-1], edges[1:]):
+        while lo < hi:
+            pieces.append((lo, min(size, hi - lo)))
+            lo += size
+    return pieces
+
+
+def cell_piece(z_ref, next_ref, c_ref, mask_ref, vec, sav_ref, lo, col, count, kept, last):
+    here = tile_rows(col, count)
+    z_here = tile_rows(col - lo, count)
+    c_old = c_ref[here, :]
+    gate_in = gate(z_ref[z_here, 0:128] + vec[0] + vec[4] * c_old)
+    gate_keep = gate(z_ref[z_here, 128:256] + vec[1] + vec[5] * c_old)
+    cand = jnp.tanh(z_ref[z_here, 256:384] + vec[2])
+    c_new = mask_ref[here, :] * (gate_keep * c_old + gate_in * cand)
+    gate_out = gate(z_ref[z_here, 384:512] + vec[3] + vec[6] * c_new)
+    h_new = gate_out * jnp.tanh(c_new)
+    c_ref[here, :] = c_new
+    above, below = row_moves(h_new)
+    next_ref[here, 0:128] = above.astype(bf16)
+    next_ref[here, 128:256] = h_new.astype(bf16)
+    next_ref[here, 256:384] = below.astype(bf16)
+    if kept <= col < last:
+        slot = tile_rows(col - kept, count)
+        sav_ref[0, slot, 0:128] = gate_in
+        sav_ref[0, slot, 128:256] = gate_keep
+        sav_ref[0, slot, 256:384] = cand
+        sav_ref[0, slot, 384:512] = gate_out
+        sav_ref[0, slot, 512:640] = c_old
+
+
+def forward_step(refs, lo, hi, size, kept, last, conv, aside=None):
+    z_ref, h3_ref, next_ref, c_ref, mask_ref, vec_ref, sav_ref = refs
+    vec = [vec_ref[k : k + 1, :] for k in range(7)]
+
+    def cell_of(col, count):
+        for piece in cuts(col, col + count, 4, (kept, last)):
+            cell_piece(z_ref, next_ref, c_ref, mask_ref, vec, sav_ref, lo, *piece, kept, last)
+
+    waiting = None
+    pieces = cuts(lo, hi, size)
+    for k, piece in enumerate(pieces):
+        conv(*piece)
+        if aside is not None:
+            aside(k, len(pieces))
+        if waiting is not None:
+            cell_of(*waiting)
+        waiting = piece
+    cell_of(*waiting)
+    h3_ref[tile_rows(lo, hi - lo), :] = next_ref[tile_rows(lo, hi - lo), :]
+
+
+def hidden_conv(h3_ref, w_ref, z_ref, lo, extra=None, x_lo=0):
+    def conv(col, count):
+        taps = [h3_ref[tile_rows(col + b - 1, count), :] for b in range(3)]
+        z = jnp.dot(jnp.concatenate(taps, axis=1), w_ref[...], preferred_element_type=f32)
+        if extra is not None:
+            x_ref, wx_ref = extra
+            z = z + jnp.dot(
+                x_ref[tile_rows(col - x_lo, count), :], wx_ref[...], preferred_element_type=f32
+            )
+        z_ref[tile_rows(col - lo, count), :] = z
+
+    return conv
+
+
+def fill_forward(w_ref, wt_ref):
+    for b in range(3):
+        for a in range(3):
+            lanes = slice((3 * a + b) * HID, (3 * a + b + 1) * HID)
+            wt_ref[(3 * b + a) * HID : (3 * b + a + 1) * HID, :] = w_ref[:, lanes].T
+
+
+def frame_parts(frame):
+    rest = 2048 - PIECE_LANES
+    return ((0, 2 * frame, 0, PIECE_LANES), (PIECE_LANES, 10 + frame // 2 * 2, frame % 2 * rest, rest))
+
+
+def pack_kernel(w_ref, wx_ref, frames_ref, vec_ref, out_ref, block_ref):
+    share = w_ref.shape[0]
+    out_ref[0:share, 0:1152] = w_ref[...].astype(bf16)
+    out_ref[0:share, 1152:1408] = jnp.zeros((share, 256), bf16)
+    out_ref[0:share, 1152:1296] = wx_ref[...].astype(bf16)
+    block_ref[...] = jnp.zeros_like(block_ref)
+    count = vec_ref.shape[1]
+    block_ref[0:1, 768 : 768 + count] = vec_ref[...]
+    near, far = block_ref[0:1, 768:896], block_ref[0:1, 896:1024]
+    lane = lax.broadcasted_iota(jnp.int32, near.shape, 1)
+    shift = HID - count // 2
+    block_ref[14:15, 640:768] = near
+    block_ref[15:16, 640:768] = jnp.where(lane < shift, pltpu.roll(near, shift, 1), pltpu.roll(far, shift, 1))
+    for frame in range(FRAMES_IN):
+        for lane, row, place, count in frame_parts(frame):
+            block_ref[row : row + 2, place : place + count] = frames_ref[frame, :, lane : lane + count].astype(f32)
+    out_ref[share : share + block_ref.shape[0], :] = block_ref[...].astype(bf16)
+
+
+def copy_windows(cot_ref, frame, out_ref, place, reach):
+    width = STRIP + 2 * reach
+    for band in range(8):
+        lo = STRIP * band - reach
+        first, last = max(lo, 0), min(lo + width, 128)
+        out_ref[band, place + first - lo : place + last - lo] = cot_ref[frame, first:last]
+        if first > lo:
+            out_ref[band, place : place + first - lo] = cot_ref[frame, 0 : first - lo]
+        if last < lo + width:
+            out_ref[band, place + last - lo : place + width] = cot_ref[frame, 0 : lo + width - last]
+
+
+def windows_kernel(cot_ref, first_ref, second_ref):
+    for k in range(2):
+        copy_windows(cot_ref, 4 - k, first_ref, KEPT * k, REACH)
+    for k in range(FRAMES_IN):
+        copy_windows(cot_ref, 2 * FRAMES_IN + k, first_ref, KEPT * (2 + k), REACH)
+        copy_windows(cot_ref, FRAMES_IN + k, first_ref, MID_COLS * (MID_PLACE + k), REACH_MID)
+    for k in range(3):
+        copy_windows(cot_ref, 2 - k, second_ref, KEPT * (SECOND_PLACE + k), REACH)
+
+
+def fill_frames(lim_ref, mine_ref, other_ref, line_ref, vec_ref, wide_ref, pairs_ref, pair_ref):
+    core_here = lax.axis_index("core")
+    wide_ref[...] = jnp.zeros_like(wide_ref)
+    pair_ref[...] = jnp.zeros_like(pair_ref)
+    for k in range(4):
+        chip = (lax.axis_index("z") - k) & 3
+        for source, core in ((mine_ref, core_here), (other_ref, 1 - core_here)):
+            band = 2 * chip + core
+            first = k * PIECE_ROWS + HID // 2
+            block = source[first : first + 16, :].astype(f32)
+            for frame in range(FRAMES_IN):
+                for lane, row, place, count in frame_parts(frame):
+                    start = OWN * 16 + lane
+                    wide_ref[band, frame, :, start : start + count] = block[row : row + 2, place : place + count]
+            pairs_ref[band] = block[14:16, 640 : 640 + HID]
+    for band in range(8):
+        pair_ref[2 * band : 2 * band + 2, :] = pairs_ref[band]
+    lanes = FRAME_COLS * 16
+    row = lax.broadcasted_iota(jnp.int32, (GRID_ROWS, lanes), 0)
+    col = (lax.broadcasted_iota(jnp.int32, (GRID_ROWS, lanes), 1) >> 4) + (own_column() - OWN)
+    inside = (row < lim_ref[0, 0]) & (col >= 0) & (col < lim_ref[0, 1])
+    start = pl.multiple_of(16 * own_column(), 256)
+    for frame in range(FRAMES_IN):
+        for band in range(8):
+            line_ref[frame, 1, 2 * band : 2 * band + 2, :] = wide_ref[band, frame, :, pl.ds(start, lanes)]
+        field = jnp.where(inside, line_ref[frame, 1], 0.0)
+        above, below = row_moves(field)
+        line_ref[frame, 0] = above
+        line_ref[frame, 1] = field
+        line_ref[frame, 2] = below
+    lane = lax.broadcasted_iota(jnp.int32, (1, HID), 1)
+    for k in range(14):
+        at, offset = divmod(HID * k, 112)
+        line = pltpu.roll(pair_ref[at : at + 1, :], (HID - offset) % HID, 1)
+        filled = 112 - offset
+        follow = pltpu.roll(pair_ref[at + 1 : at + 2, :], filled, 1)
+        line = jnp.where(lane < filled, line, follow)
+        if filled + 112 < HID:
+            third = pltpu.roll(pair_ref[at + 2 : at + 3, :], (filled + 112) % HID, 1)
+            line = jnp.where(lane < filled + 112, line, third)
+        place = k + k // 7
+        vec_ref[place : place + 1, :] = line
+    vec_ref[7:8, :] = jnp.zeros((1, HID), f32)
+    vec_ref[15:16, :] = jnp.zeros((1, HID), f32)
+
+
+def taps_of(line_ref, frame, out_ref, first, count):
+    lane = lax.broadcasted_iota(jnp.int32, (GRID_ROWS, 128), 1)
+    for col in range(first, first + count):
+        block, offset = divmod(16 * (col - 1), 128)
+        pieces = []
+        for a in range(3):
+            line = line_ref[frame, a, :, 128 * block : 128 * block + 128]
+            if offset + 48 > 128:
+                line = jnp.where(
+                    lane >= offset, line, line_ref[frame, a, :, 128 * block + 128 : 128 * block + 256]
+                )
+            pieces.append(pltpu.roll(line, ((64 if a == 1 else 0) - offset) % 128, 1))
+        left = jnp.where(lane < 48, pieces[0], jnp.where((lane >= 64) & (lane < 112), pieces[1], 0.0))
+        right = jnp.where(lane < 48, pieces[2], 0.0)
+        place = tile_rows(col - ENC_COLS[0], 1)
+        out_ref[place, 0:128] = left.astype(bf16)
+        out_ref[place, 128:256] = right.astype(bf16)
+
+
+def assemble(mine_ref, other_ref, w_ref, wx_ref=None):
+    part = HID // 2
+    core_here = lax.axis_index("core")
+    for k in range(4):
+        chip = (lax.axis_index("z") - k) & 3
+        for source, core in ((mine_ref, core_here), (other_ref, 1 - core_here)):
+            place = pl.ds(pl.multiple_of((2 * chip + core) * part, part), part)
+            first = k * (source.shape[0] // 4)
+            w_ref[place, :] = source[first : first + part, 0:1152]
+            if wx_ref is not None:
+                wx_ref[place, :] = source[first : first + part, 1152:1408]
+
+
+def enc_kernel(
+    lim_ref, mine_ref, other_ref, move_f_ref, move_b_ref,
+    sav_ref, h3s_ref, own_ref, h3_ref, c_ref, w_ref, wxb_ref, vec_ref,
+    wt_ref, wx_ref, wxt_ref, z_ref, next_ref, mask_ref, line_ref, taps_ref, taps_next, wide_ref, pairs_ref, pair_ref,
+):
+    step_id = pl.program_id(0)
+    lo, hi = ENC_COLS
+    kept = OWN - ENC_REACH
+    last = kept + ENC_KEPT
+    refs = (z_ref, h3_ref, next_ref, c_ref, mask_ref, vec_ref, sav_ref)
+
+    @pl.when(step_id == 0)
+    def _():
+        h3_ref[...] = jnp.zeros_like(h3_ref)
+        c_ref[...] = jnp.zeros_like(c_ref)
+        fill_mask(lim_ref, mask_ref, -OWN)
+        fill_frames(lim_ref, mine_ref, other_ref, line_ref, vec_ref, wide_ref, pairs_ref, pair_ref)
+        assemble(mine_ref, other_ref, w_ref, wx_ref)
+        fill_forward(w_ref, wt_ref)
+        wx = wx_ref[...]
+        wxt_ref[...] = lax.dot_general(
+            move_f_ref[...], wx, (((0,), (1,)), ((), ())), preferred_element_type=f32
+        ).astype(bf16)
+        wxb_ref[...] = jnp.dot(wx, move_b_ref[...], preferred_element_type=f32).astype(bf16)
+        taps_of(line_ref, 0, taps_ref, lo, hi - lo)
+
+    own_ref[0] = taps_ref[tile_rows(OWN - lo, STRIP), :]
+
+    def next_taps(k, parts):
+        pieces = cuts(lo, hi, -(-(hi - lo) // parts))
+        taps_of(line_ref, jnp.minimum(step_id + 1, FRAMES_IN - 1), taps_next, *pieces[k])
+
+    @pl.when(step_id == 0)
+    def _():
+        def conv(col, count):
+            here = tile_rows(col - lo, count)
+            z_ref[here, :] = jnp.dot(taps_ref[here, :], wxt_ref[...], preferred_element_type=f32)
+
+        forward_step(refs, lo, hi, 25, kept, last, conv, next_taps)
+
+    @pl.when(step_id > 0)
+    def _():
+        h3s_ref[0] = h3_ref[pl.ds((OWN - 1) * GRID_ROWS, (STRIP + 2) * GRID_ROWS), :]
+
+    def run(_, halo, piece):
+        first, end = OWN - halo, OWN + STRIP + halo
+        conv = hidden_conv(h3_ref, wt_ref, z_ref, first, (taps_ref, wxt_ref), lo)
+        forward_step(refs, first, end, piece, kept, last, conv, next_taps)
+
+    runs_of(ENC_RUNS, FRAMES_IN, step_id, run)
+    taps_ref[...] = taps_next[...]
+
+
+def fore_kernel(
+    lim_ref, mine_ref, other_ref, vec_ref, h3_in, c_in, order_ref, out_in,
+    sav_ref, mid_ref, h3s_ref, out_ref, w_ref, h3_ref, c_ref, wt_ref, z_ref, next_ref, mask_ref,
+):
+    step_id = pl.program_id(0)
+
+    @pl.when(step_id == 0)
+    def _():
+        h3_ref[...] = h3_in[...]
+        c_ref[...] = c_in[...]
+        fill_mask(lim_ref, mask_ref, -OWN)
+        assemble(mine_ref, other_ref, w_ref)
+        fill_forward(w_ref, wt_ref)
+
+    h3s_ref[0] = h3_ref[pl.ds((OWN - 1) * GRID_ROWS, (STRIP + 2) * GRID_ROWS), :]
+
+    def run(first, halo, piece):
+        middle = FRAMES_IN <= first < 2 * FRAMES_IN
+        reach = REACH_MID if middle else REACH
+        save = mid_ref if middle else sav_ref
+        refs = (z_ref, h3_ref, next_ref, c_ref, mask_ref, vec_ref, save)
+        lo, hi = OWN - halo, OWN + STRIP + halo
+        conv = hidden_conv(h3_ref, wt_ref, z_ref, lo)
+        forward_step(refs, lo, hi, piece, OWN - reach, OWN + STRIP + reach, conv)
+
+    runs_of(FORE_RUNS, FRAMES_OUT, step_id, run)
+    own = h3_ref[pl.ds(OWN * GRID_ROWS, STRIP * GRID_ROWS), 128:256]
+    rows = jnp.dot(order_ref[...], own, preferred_element_type=f32).astype(bf16)
+    for band in range(8):
+        out_ref[band] = rows[32 * band : 32 * band + 32]
+
+
+def join_kernel(got_ref, out_ref):
+    for band in range(8):
+        for k in range(3):
+            out_ref[k, 32 * band : 32 * band + 32] = got_ref[band, 32 * k : 32 * k + 32]
+
+
+def back_piece(refs, vec, col, count, own, kept):
+    sav_ref, og_ref, dh_ref, dc_ref, d_ref, mask_ref, sum_ref = refs
+    here = tile_rows(col, count)
+    then = tile_rows(col - kept, count)
+    gate_in = sav_ref[0, then, 0:128]
+    gate_keep = sav_ref[0, then, 128:256]
+    cand = sav_ref[0, then, 256:384]
+    gate_out = sav_ref[0, then, 384:512]
+    c_old = sav_ref[0, then, 512:640]
+    mask = mask_ref[here, :]
+    dh = dh_ref[here, :]
+    if og_ref is not None:
+        dh = dh + og_ref[then, :].astype(f32)
+    c_new = mask * (gate_keep * c_old + gate_in * cand)
+    bent = jnp.tanh(c_new)
+    dz_out = dh * bent * gate_out * (1.0 - gate_out)
+    dc = dc_ref[here, :] + dh * gate_out * (1.0 - bent * bent) + dz_out * vec[6]
+    dc = dc * mask
+    dz_in = dc * cand * gate_in * (1.0 - gate_in)
+    dz_keep = dc * c_old * gate_keep * (1.0 - gate_keep)
+    dz_cand = dc * gate_in * (1.0 - cand * cand)
+    dc_ref[here, :] = dc * gate_keep + dz_in * vec[4] + dz_keep * vec[5]
+    slot = tile_rows(col + 1, count)
+    d_ref[slot, 0:128] = dz_in.astype(bf16)
+    d_ref[slot, 128:256] = dz_keep.astype(bf16)
+    d_ref[slot, 256:384] = dz_cand.astype(bf16)
+    d_ref[slot, 384:512] = dz_out.astype(bf16)
+    if own:
+        terms = (dz_in, dz_keep, dz_cand, dz_out, dz_in * c_old, dz_keep * c_old, dz_out * c_new)
+        for k, term in enumerate(terms):
+            sum_ref[8 * k : 8 * k + 8, :] += jnp.sum(term.reshape(-1, 8, 128), axis=0)
+
+
+def back_conv(d_ref, w_ref, dh_ref, col, count, wxb_ref=None, qx_ref=None):
+    q = None
+    for b in range(3):
+        blocks = [w_ref[:, (3 * a + b) * HID : (3 * a + b + 1) * HID] for a in range(3)]
+        if wxb_ref is not None:
+            blocks.append(wxb_ref[:, b * HID : (b + 1) * HID])
+        term = jnp.dot(
+            d_ref[tile_rows(col + 2 - b, count), :],
+            jnp.concatenate(blocks, axis=1),
+            preferred_element_type=f32,
+        )
+        q = term if q is None else q + term
+    down, _ = row_moves(q[:, 256:384])
+    _, up = row_moves(q[:, 0:128])
+    dh_ref[tile_rows(col, count), :] = up + q[:, 128:256] + down
+    if wxb_ref is not None:
+        qx_ref[tile_rows(col, count), :] = q[:, 384:512]
+
+
+def spread(d_ref, w_ref, part_ref, col, count):
+    part_ref[tile_rows(col, count), :] = jnp.dot(
+        d_ref[tile_rows(col + 1, count), :], w_ref[...], preferred_element_type=f32
+    )
+
+
+def collect(part_ref, dh_ref, first, last, lo, hi):
+    for col, count in cuts(first, last, 4, (lo + 1, hi - 1)):
+        rows = []
+        for a in range(3):
+            total = None
+            for b in range(3):
+                source = col + 1 - b
+                if source < lo or source + count > hi:
+                    continue
+                lanes = slice((3 * a + b) * HID, (3 * a + b + 1) * HID)
+                term = part_ref[tile_rows(source, count), lanes]
+                total = term if total is None else total + term
+            rows.append(total)
+        _, up = row_moves(rows[0])
+        down, _ = row_moves(rows[2])
+        dh_ref[tile_rows(col, count), :] = up + rows[1] + down
+
+
+def spread_step(refs, vec_ref, w_ref, part_ref, lo, hi, own, size, kept=0):
+    dh_ref, d_ref = refs[2], refs[4]
+    vec = [vec_ref[k : k + 1, :] for k in range(7)]
+    pieces = cuts(lo, hi, size)
+    done = lo
+    for k, (col, count) in enumerate(pieces):
+        for place, width in cuts(col, col + count, 4, (own, own + STRIP)):
+            back_piece(refs, vec, place, width, own <= place < own + STRIP, kept)
+        if k > 0:
+            collect(part_ref, dh_ref, done, col - 1, lo, hi)
+            done = col - 1
+        spread(d_ref, w_ref, part_ref, col, count)
+    collect(part_ref, dh_ref, done, hi, lo, hi)
+
+
+def backward_step(refs, vec_ref, w_ref, lo, hi, own, size, kept=0, extra=()):
+    dh_ref, d_ref = refs[2], refs[4]
+    vec = [vec_ref[k : k + 1, :] for k in range(7)]
+    pieces = cuts(lo, hi, size)
+    done = lo
+    for k, (col, count) in enumerate(pieces):
+        last = min(col + count + 1, hi)
+        for place, width in cuts(done, last, 4, (own, own + STRIP)):
+            back_piece(refs, vec, place, width, own <= place < own + STRIP, kept)
+        done = last
+        if k > 0:
+            back_conv(d_ref, w_ref, dh_ref, *pieces[k - 1], *extra)
+    back_conv(d_ref, w_ref, dh_ref, *pieces[-1], *extra)
+
+
+def across(d_turned, fields):
+    return jnp.dot(d_turned, fields, preferred_element_type=f32)
+
+
+def turn(d_ref, first, out_ref):
+    for g in range(4):
+        out_ref[HID * g : HID * (g + 1), :] = d_ref[tile_rows(first, STRIP), HID * g : HID * (g + 1)].T
+
+
+def side_rows(h3s_ref, frames):
+    return jnp.concatenate(
+        [
+            jnp.concatenate([h3s_ref[k, tile_rows(b, STRIP), :] for k in frames], axis=0)
+            for b in range(3)
+        ],
+        axis=1,
+    )
+
+
+def split_by_core(value, lanes, keep_ref, send_ref):
+    share = value.shape[0] // 4
+    core = lax.axis_index("core")
+    for band in range(4):
+        rows = value[band * share : (band + 1) * share]
+        place = pl.ds(band // 2 * share, share)
+
+        @pl.when(core == band % 2)
+        def _(rows=rows, place=place):
+            keep_ref[place, lanes] = rows
+
+        @pl.when(core != band % 2)
+        def _(rows=rows, place=place):
+            send_ref[place, lanes] = rows
+
+
+OWN_CELLS = pl.ds(REACH * GRID_ROWS, STRIP * GRID_ROWS)
+EDGE_CELLS = REACH * GRID_ROWS
+
+
+def back_late_kernel(
+    lim_ref, w_ref, vec_ref, sav_ref, og_ref, mid_ref, og_mid_ref,
+    d_out, sum_ref, dh_out, dc_out, left_ref, right_ref, dh_ref, dc_ref, d_ref, mask_ref, part_ref,
+):
+    step_id = pl.program_id(0)
+
+    @pl.when(step_id == 0)
+    def _():
+        for ref in (d_ref, dh_ref, dc_ref, sum_ref):
+            ref[...] = jnp.zeros_like(ref)
+        fill_mask(lim_ref, mask_ref, -REACH)
+
+    rest = (dh_ref, dc_ref, d_ref, mask_ref, sum_ref)
+
+    def run(first, halo, piece):
+        lo, hi = REACH - halo, REACH + STRIP + halo
+        if first < FRAMES_IN:
+            spread_step((sav_ref, og_ref, *rest), vec_ref, w_ref, part_ref, lo, hi, REACH, piece)
+        else:
+            kept = REACH - REACH_MID
+            spread_step((mid_ref, og_mid_ref, *rest), vec_ref, w_ref, part_ref, lo, hi, REACH, piece, kept)
+
+    runs_of(LATE_RUNS, 2 * FRAMES_IN, step_id, run)
+    turn(d_ref, REACH + 1, d_out)
+
+    @pl.when(step_id == 2 * FRAMES_IN - 1)
+    def _():
+        for k, (ref, out) in enumerate(((dh_ref, dh_out), (dc_ref, dc_out))):
+            out[...] = ref[OWN_CELLS, :]
+            left_ref[k] = ref[pl.ds(REACH * GRID_ROWS, EDGE_CELLS), :].astype(bf16)
+            right_ref[k] = ref[pl.ds(STRIP * GRID_ROWS, EDGE_CELLS), :].astype(bf16)
+
+
+def back_early_kernel(
+    lim_ref, w_ref, vec_ref, sav_ref, og_ref, og_next, sum_in, dh_in, dc_in, left_in, right_in,
+    d_out, sum_ref, dh_ref, dc_ref, d_ref, mask_ref, part_ref,
+):
+    step_id = pl.program_id(0)
+
+    @pl.when(step_id == 0)
+    def _():
+        d_ref[...] = jnp.zeros_like(d_ref)
+        for k, (ref, own) in enumerate(((dh_ref, dh_in), (dc_ref, dc_in))):
+            ref[pl.ds(0, EDGE_CELLS), :] = left_in[k].astype(f32)
+            ref[OWN_CELLS, :] = own[...]
+            ref[pl.ds((REACH + STRIP) * GRID_ROWS, EDGE_CELLS), :] = right_in[k].astype(f32)
+        sum_ref[...] = sum_in[...]
+        fill_mask(lim_ref, mask_ref, -REACH)
+
+    def run(first, halo, piece):
+        og = og_ref if first < 2 else og_next
+        refs = (sav_ref, og, dh_ref, dc_ref, d_ref, mask_ref, sum_ref)
+        spread_step(refs, vec_ref, w_ref, part_ref, REACH - halo, REACH + STRIP + halo, REACH, piece)
+
+    runs_of(EARLY_RUNS, FRAMES_IN, step_id, run)
+    turn(d_ref, REACH + 1, d_out)
+
+
+def enc_back_kernel(
+    lim_ref, w_ref, wxb_ref, vec_ref, sav_ref, dh_in, dc_in,
+    d_out, dx_ref, sum_ref, dh_ref, dc_ref, d_ref, mask_ref, qx_ref,
+):
+    step_id = pl.program_id(0)
+    edge = REACH - ENC_REACH
+
+    @pl.when(step_id == 0)
+    def _():
+        dh_ref[...] = dh_in[pl.ds(edge * GRID_ROWS, ENC_KEPT * GRID_ROWS), :]
+        dc_ref[...] = dc_in[pl.ds(edge * GRID_ROWS, ENC_KEPT * GRID_ROWS), :]
+        for ref in (d_ref, sum_ref, qx_ref):
+            ref[...] = jnp.zeros_like(ref)
+        fill_mask(lim_ref, mask_ref, -ENC_REACH)
+
+    refs = (sav_ref, None, dh_ref, dc_ref, d_ref, mask_ref, sum_ref)
+
+    def run(_, halo, piece):
+        lo, hi = ENC_REACH - halo, ENC_REACH + STRIP + halo
+        backward_step(refs, vec_ref, w_ref, lo, hi, ENC_REACH, piece, 0, (wxb_ref, qx_ref))
+
+    runs_of(ENC_BACK_RUNS, FRAMES_IN, step_id, run)
+    turn(d_ref, ENC_REACH + 1, d_out)
+    own = tile_rows(ENC_REACH, STRIP)
+    qx = qx_ref[own, :]
+    down, up = row_moves(qx)
+    total = up + pltpu.roll(qx, HID - 16, 1) + pltpu.roll(down, HID - 32, 1)
+    total = total * mask_ref[own, :]
+    lane = lax.broadcasted_iota(jnp.int32, total.shape, 1)
+    total = jnp.where(lane < 16, total, 0.0)
+    for group in range(2):
+        line = jnp.zeros((GRID_ROWS, 128), f32)
+        for k in range(8):
+            place = (8 * group + k) * GRID_ROWS
+            line = line + pltpu.roll(total[place : place + GRID_ROWS], 16 * k, 1)
+        dx_ref[0, :, 128 * group : 128 * group + 128] = line
+
+
+LATE = tuple(range(FRAMES_IN, FRAMES_OUT))
+EARLY = tuple(range(FRAMES_IN))
+
+
+def late_sums_kernel(dt_ref, h3s_ref, g_ref):
+    g_ref[...] = across(dt_ref[...], side_rows(h3s_ref, LATE))
+
+
+def put_sums(g, keep_ref, send_ref):
+    for a in range(3):
+        for b in range(3):
+            lanes = slice((3 * a + b) * HID, (3 * a + b + 1) * HID)
+            split_by_core(g[:, (3 * b + a) * HID : (3 * b + a + 1) * HID], lanes, keep_ref, send_ref)
+
+
+def early_sums_kernel(dt_ref, h3s_ref, g_in, keep_ref, send_ref):
+    g = g_in[...] + across(dt_ref[...], side_rows(h3s_ref, EARLY))
+    put_sums(g.astype(bf16), keep_ref, send_ref)
+
+
+def enc_sums_kernel(dt_ref, h3s_ref, x_ref, move_ref, sum_ref, sum_in, keep_ref, send_ref):
+    g = across(dt_ref[:, 256:], side_rows(h3s_ref, EARLY[1:]))
+    put_sums(g.astype(bf16), keep_ref, send_ref)
+
+    fields = jnp.concatenate([x_ref[k] for k in EARLY], axis=0)
+    gx = lax.dot_general(
+        across(dt_ref[...], fields).astype(bf16),
+        move_ref[...],
+        (((1,), (1,)), ((), ())),
+        preferred_element_type=f32,
+    )
+    lines = [
+        jnp.sum(ref[8 * k : 8 * k + 8, :], axis=0, keepdims=True)
+        for ref in (sum_ref, sum_in)
+        for k in range(7)
+    ] + [jnp.zeros((1, HID), f32)]
+    lane = lax.broadcasted_iota(jnp.int32, (1, HID), 1)
+    rows = []
+    for k in range(16):
+        at, offset = divmod(112 * k, HID)
+        line = jnp.where(lane >= offset, lines[at], lines[at + 1])
+        rows.append(jnp.where(lane >= 16, pltpu.roll(line, (16 - offset) % HID, 1), 0.0))
+    rows = jnp.concatenate(rows, axis=0)
+    gx = jnp.concatenate([gx[:, :128], gx[:, 128:] + jnp.concatenate([rows] * 16, axis=0)], axis=1)
+    split_by_core(gx.astype(bf16), slice(1152, 1408), keep_ref, send_ref)
+
+
+def whole_spec(array):
+    return pl.BlockSpec(array.shape, lambda i: (0,) * len(array.shape))
+
+
+def step_spec(shape, last=None):
+    if last is None:
+        return pl.BlockSpec((1, *shape), lambda i: (i, 0, 0))
+    return pl.BlockSpec((1, *shape), lambda i: (last - i, 0, 0))
+
+
+SMEM_SPEC = pl.BlockSpec(memory_space=pltpu.SMEM)
+
+
+def cost(steps, columns, passes):
+    return pl.CostEstimate(
+        flops=2 * steps * columns * GRID_ROWS * 1152 * 512 * passes,
+        bytes_accessed=steps * 2 * 1024 * 1024,
+        transcendentals=steps * columns * GRID_ROWS * 128 * 5,
+    )
+
+
+def shaped(shape, dtype):
+    return jax.ShapeDtypeStruct(shape, dtype)
+
+
+FULL = FRAME_COLS * GRID_ROWS
+SIDE = (STRIP + 2) * GRID_ROWS
+ENC_WIDTH = (ENC_COLS[1] - ENC_COLS[0]) * GRID_ROWS
+ENC_CELLS = ENC_KEPT * GRID_ROWS
+CELLS = KEPT * GRID_ROWS
+MID_COLS = STRIP + 2 * REACH_MID
+MID_CELLS = MID_COLS * GRID_ROWS
+MID_PLACE = 10
+SECOND_PLACE = 7
+FIRST_COLS = MID_COLS * (MID_PLACE + FRAMES_IN)
+SECOND_COLS = KEPT * (SECOND_PLACE + 3)
+
+
+def held(shape, dtype):
+    return pltpu.HBM(shape, dtype)
+
+
+def call(kernel, name, grid, ins, outs, scratch, estimate, aliases=None, memory=LARGE):
+    def spec(pair):
+        array, block = pair
+        return whole_spec(array) if block is None else block
+
+    return pl.pallas_call(
+        kernel,
+        grid=(grid,),
+        in_specs=[spec(pair) for pair in ins],
+        out_specs=[spec(pair) for pair in outs],
+        out_shape=[pair[0] for pair in outs],
+        scratch_shapes=scratch,
+        compiler_params=pltpu.CompilerParams(
+            dimension_semantics=("arbitrary",), vmem_limit_bytes=memory * MIB
+        ),
+        cost_estimate=estimate,
+        input_output_aliases=aliases or {},
+        name=name,
+    )(*[pair[0] for pair in ins])
+
+
+def moves():
+    forward = np.zeros((256, 256), np.float32)
+    backward = np.zeros((256, 384), np.float32)
+    for a in range(3):
+        for b in range(3):
+            for k in range(16):
+                forward[(3 * a + b) * 16 + k, 64 * a + 16 * b + k] = 1.0
+                backward[(3 * a + b) * 16 + k, 128 * b + 16 * a + k] = 1.0
+    return jnp.asarray(forward, bf16), jnp.asarray(backward, bf16)
+
+
+ANY_SPEC = pl.BlockSpec(memory_space=pl.ANY)
+
+
+def pack_parts(weight, weight_x, frames, vec):
+    return call(
+        pack_kernel,
+        "pack_parts",
+        1,
+        [(weight, None), (weight_x, None), (frames, None), (vec, None)],
+        [(shaped((PIECE_ROWS, 1408), bf16), None)],
+        [pltpu.VMEM((16, PIECE_LANES), f32)],
+        pl.CostEstimate(flops=0, bytes_accessed=0, transcendentals=0),
+    )[0]
+
+
+def cot_windows(cot):
+    return call(
+        windows_kernel,
+        "cot_windows",
+        1,
+        [(cot, None)],
+        [
+            (shaped((8, FIRST_COLS, 2, HID), bf16), None),
+            (shaped((8, SECOND_COLS, 2, HID), bf16), None),
+        ],
+        [],
+        pl.CostEstimate(flops=0, bytes_accessed=0, transcendentals=0),
+    )
+
+
+def forward_enc(lim, mine, other):
+    move_f, move_b = moves()
+    wide = (OWN + 128 + FRAME_COLS - OWN) * 16
+    return call(
+        enc_kernel,
+        "enc_forward",
+        FRAMES_IN,
+        [
+            (lim, SMEM_SPEC),
+            (mine, None),
+            (other, None),
+            (move_f, None),
+            (move_b, None),
+        ],
+        [
+            (held((FRAMES_IN, ENC_CELLS, 640), f32), step_spec((ENC_CELLS, 640))),
+            (held((FRAMES_IN, SIDE, 384), bf16), step_spec((SIDE, 384))),
+            (
+                held((FRAMES_IN, STRIP * GRID_ROWS, 256), bf16),
+                step_spec((STRIP * GRID_ROWS, 256)),
+            ),
+            (held((FULL, 384), bf16), None),
+            (held((FULL, 128), f32), None),
+            (held((512, 1152), bf16), None),
+            (held((512, 384), bf16), None),
+            (held((16, 128), f32), None),
+        ],
+        [
+            pltpu.VMEM((1152, 512), bf16),
+            pltpu.VMEM((512, 256), bf16),
+            pltpu.VMEM((256, 512), bf16),
+            pltpu.VMEM((ENC_WIDTH, 512), f32),
+            pltpu.VMEM((FULL, 384), bf16),
+            pltpu.VMEM((FULL, 128), f32),
+            pltpu.VMEM((FRAMES_IN, 3, GRID_ROWS, FRAME_COLS * 16), f32),
+            pltpu.VMEM((ENC_WIDTH, 256), bf16),
+            pltpu.VMEM((ENC_WIDTH, 256), bf16),
+            pltpu.VMEM((8, FRAMES_IN, 2, wide), f32),
+            pltpu.VMEM((8, 2, HID), f32),
+            pltpu.VMEM((24, HID), f32),
+        ],
+        cost(FRAMES_IN, 72, 1),
+        memory=LONG,
+    )
+
+
+def row_order():
+    order = np.zeros((256, 256), np.float32)
+    for col in range(STRIP):
+        for row in range(GRID_ROWS):
+            order[row // 2 * 32 + col * 2 + row % 2, col * GRID_ROWS + row] = 1.0
+    return jnp.asarray(order, bf16)
+
+
+def forward_fore(lim, mine, other, vec, h3, state, second):
+    second = second.reshape(8, SECOND_COLS * 2, HID)
+    return call(
+        fore_kernel,
+        "fore_forward",
+        FRAMES_OUT,
+        [
+            (lim, SMEM_SPEC),
+            (mine, None),
+            (other, None),
+            (vec, None),
+            (h3, None),
+            (state, None),
+            (row_order(), None),
+            (second, ANY_SPEC),
+        ],
+        [
+            (
+                held((2 * FRAMES_IN, CELLS, 640), f32),
+                pl.BlockSpec(
+                    (1, CELLS, 640),
+                    lambda i: (jnp.where(i < FRAMES_IN, i, jnp.maximum(i - FRAMES_IN, FRAMES_IN - 1)), 0, 0),
+                ),
+            ),
+            (
+                held((FRAMES_IN, MID_CELLS, 640), f32),
+                pl.BlockSpec((1, MID_CELLS, 640), lambda i: (jnp.clip(i - FRAMES_IN, 0, FRAMES_IN - 1), 0, 0)),
+            ),
+            (held((FRAMES_OUT, SIDE, 384), bf16), step_spec((SIDE, 384))),
+            (
+                shaped(second.shape, bf16),
+                pl.BlockSpec((8, 2 * STRIP, HID), lambda i: (0, i, 0)),
+            ),
+            (held((512, 1152), bf16), None),
+        ],
+        [
+            pltpu.VMEM((FULL, 384), bf16),
+            pltpu.VMEM((FULL, 128), f32),
+            pltpu.VMEM((1152, 512), bf16),
+            pltpu.VMEM((64 * GRID_ROWS, 512), f32),
+            pltpu.VMEM((FULL, 384), bf16),
+            pltpu.VMEM((FULL, 128), f32),
+        ],
+        cost(FRAMES_OUT, 56, 1),
+        {7: 3},
+        LONG,
+    )
+
+
+def join_hidden(got):
+    out = call(
+        join_kernel,
+        "join_hidden",
+        FRAMES_IN,
+        [(got, pl.BlockSpec((8, 6 * STRIP, HID), lambda i: (0, i, 0)))],
+        [
+            (
+                shaped((FRAMES_OUT, 2 * STRIP * 8, HID), bf16),
+                pl.BlockSpec((3, 2 * STRIP * 8, HID), lambda i: (i, 0, 0)),
+            )
+        ],
+        [],
+        pl.CostEstimate(flops=0, bytes_accessed=1 << 21, transcendentals=0),
+        memory=SMALL,
+    )[0]
+    out = out.reshape(FRAMES_OUT, STRIP * 8, 2, HID).transpose(0, 2, 1, 3)
+    return out.reshape(1, FRAMES_OUT, 2, -1)
+
+
+def tile_spec(cols, place):
+    return pl.BlockSpec((cols * GRID_ROWS, HID), lambda i: (place(i), 0))
+
+
+D_SHAPE = (512, STRIP * GRID_ROWS)
+
+
+def turned(steps):
+    return (
+        pltpu.VMEM((512, steps * STRIP * GRID_ROWS), bf16),
+        pl.BlockSpec(D_SHAPE, lambda i: (0, steps - 1 - i)),
+    )
+
+
+def backward_late(lim, weight, vec, saved, middle, og):
+    own = STRIP * GRID_ROWS
+    edge = held((2, EDGE_CELLS, 128), bf16)
+
+    def first(i):
+        return FRAMES_IN - 1 - jnp.minimum(i, FRAMES_IN - 1)
+
+    def second(i):
+        return jnp.minimum(2 * FRAMES_IN - 1 - i, FRAMES_IN - 1)
+
+    return call(
+        back_late_kernel,
+        "fore_backward_late",
+        2 * FRAMES_IN,
+        [
+            (lim, SMEM_SPEC),
+            (weight, None),
+            (vec, None),
+            (saved, pl.BlockSpec((1, CELLS, 640), lambda i: (FRAMES_IN + first(i), 0, 0))),
+            (og, tile_spec(KEPT, lambda i: 2 + first(i))),
+            (middle, pl.BlockSpec((1, MID_CELLS, 640), lambda i: (second(i), 0, 0))),
+            (og, tile_spec(MID_COLS, lambda i: MID_PLACE + second(i))),
+        ],
+        [
+            turned(2 * FRAMES_IN),
+            (held((56, 128), f32), None),
+            (held((own, 128), f32), None),
+            (held((own, 128), f32), None),
+            (edge, None),
+            (edge, None),
+        ],
+        [
+            pltpu.VMEM((CELLS, 128), f32),
+            pltpu.VMEM((CELLS, 128), f32),
+            pltpu.VMEM((CELLS + 2 * GRID_ROWS, 512), bf16),
+            pltpu.VMEM((CELLS, 128), f32),
+            pltpu.VMEM((CELLS, 1152), f32),
+        ],
+        cost(2 * FRAMES_IN, 30, 1),
+        memory=LONG,
+    )
+
+
+def backward_early(lim, weight, vec, saved, og, og_next, carried):
+    return call(
+        back_early_kernel,
+        "fore_backward_early",
+        FRAMES_IN,
+        [
+            (lim, SMEM_SPEC),
+            (weight, None),
+            (vec, None),
+            (saved, step_spec((CELLS, 640), FRAMES_IN - 1)),
+            (og, tile_spec(KEPT, lambda i: jnp.minimum(i, 1))),
+            (og_next, tile_spec(KEPT, lambda i: jnp.maximum(i - 2, 0))),
+            *[(array, None) for array in carried],
+        ],
+        [
+            turned(FRAMES_IN),
+            (held((56, 128), f32), None),
+            (held((CELLS, 128), f32), None),
+            (held((CELLS, 128), f32), None),
+        ],
+        [
+            pltpu.VMEM((CELLS + 2 * GRID_ROWS, 512), bf16),
+            pltpu.VMEM((CELLS, 128), f32),
+            pltpu.VMEM((CELLS, 1152), f32),
+        ],
+        cost(FRAMES_IN, 36, 1),
+        memory=MIDDLE,
+    )
+
+
+def backward_enc(lim, weight, weight_xb, vec, saved, dh, dc):
+    last = FRAMES_IN - 1
+    return call(
+        enc_back_kernel,
+        "enc_backward",
+        FRAMES_IN,
+        [
+            (lim, SMEM_SPEC),
+            (weight, None),
+            (weight_xb, None),
+            (vec, None),
+            (saved, step_spec((ENC_CELLS, 640), last)),
+            (dh, None),
+            (dc, None),
+        ],
+        [
+            turned(FRAMES_IN),
+            (shaped((FRAMES_IN, GRID_ROWS, 256), f32), step_spec((GRID_ROWS, 256), last)),
+            (shaped((56, 128), f32), None),
+        ],
+        [
+            pltpu.VMEM((ENC_CELLS, 128), f32),
+            pltpu.VMEM((ENC_CELLS, 128), f32),
+            pltpu.VMEM((ENC_CELLS + 2 * GRID_ROWS, 512), bf16),
+            pltpu.VMEM((ENC_CELLS, 128), f32),
+            pltpu.VMEM((ENC_CELLS, 128), f32),
+        ],
+        cost(FRAMES_IN, 28, 1),
+        memory=LONG,
+    )
+
+
+def sums_cost(frames):
+    return pl.CostEstimate(
+        flops=2 * frames * 256 * 512 * 1152, bytes_accessed=frames * 500000, transcendentals=0
+    )
+
+
+def gate_half(shape):
+    return pl.BlockSpec((shape[0] // 2, shape[1]), lambda i: (i, 0))
+
+
+def half_pair(shape, dtype):
+    return (shaped(shape, dtype), gate_half(shape))
+
+
+def late_sums(d_late, sides):
+    return call(
+        late_sums_kernel,
+        "late_sums",
+        2,
+        [(d_late, gate_half(d_late.shape)), (sides, None)],
+        [half_pair((512, 1152), f32)],
+        [],
+        sums_cost(2 * FRAMES_IN),
+        memory=SMALL,
+    )[0]
+
+
+def early_sums(d_early, sides, g_late):
+    return call(
+        early_sums_kernel,
+        "early_sums",
+        2,
+        [
+            (d_early, gate_half(d_early.shape)),
+            (sides, pl.BlockSpec((FRAMES_IN, SIDE, 384), lambda i: (0, 0, 0))),
+            (g_late, gate_half(g_late.shape)),
+        ],
+        [half_pair((256, 1152), bf16), half_pair((256, 1152), bf16)],
+        [],
+        sums_cost(FRAMES_IN),
+        memory=SMALL,
+    )
+
+
+def enc_sums(d_enc, sides, x_own, sums, fore_sums):
+    move_f, _ = moves()
+    return call(
+        enc_sums_kernel,
+        "enc_sums",
+        2,
+        [
+            (d_enc, gate_half(d_enc.shape)),
+            (sides, None),
+            (x_own, None),
+            (move_f, None),
+            (sums, None),
+            (fore_sums, None),
+        ],
+        [half_pair((256, 1408), bf16), half_pair((256, 1408), bf16)],
+        [],
+        sums_cost(FRAMES_IN),
+        memory=SMALL,
+    )
+
+
+BAND = ("z", "core")
+
+
+def column_tiles(got):
+    return got.transpose(1, 0, 2, 3).reshape(-1, HID)
+
+
+def passed(value, axis, steps):
+    count = lax.axis_size(axis)
+    return lax.ppermute(value, axis, [(k, (k + steps) % count) for k in range(count)])
+
+
+def traded(blocks):
+    chips = lax.axis_size("z")
+    here, core = lax.axis_index("z"), lax.axis_index("core")
+    pairs = blocks.reshape(chips, 2, *blocks.shape[1:])
+    keep = lax.dynamic_index_in_dim(pairs, core, 1, keepdims=False)
+    send = lax.dynamic_index_in_dim(pairs, 1 - core, 1, keepdims=False)
+    other = passed(send, "core", 1)
+    first = jnp.where(core == 0, keep, other)
+    second = jnp.where(core == 0, other, keep)
+    both = jnp.stack([first, second], axis=1)
+    both = jnp.concatenate([both, both], axis=0)
+    mine = lax.dynamic_slice_in_dim(both, here, chips)
+    got = [mine[0]] + [passed(mine[s], "z", s) for s in range(1, chips)]
+    order = jnp.stack(got[::-1] + got[::-1])
+    ordered = lax.dynamic_slice_in_dim(order, chips - 1 - here, chips)
+    return ordered.reshape(blocks.shape)
+
+
+def grid_gather(share):
+    count = lax.axis_size("grp")
+    pieces = [share] + [passed(share, "grp", -s) for s in range(1, count)]
+    place = lax.axis_index("grp")
+    start = lax.rem(count - place, count) * share.shape[0]
+    return lax.dynamic_slice_in_dim(jnp.concatenate(pieces + pieces), start, count * share.shape[0])
+
+
+def chip_sum(keep, send):
+    return (keep.astype(f32) + passed(send, "core", 1).astype(f32)).astype(bf16)
+
+
+def slice_sum(total):
+    chips = lax.axis_size("z") * lax.axis_size("grp")
+    blocks = total.reshape(chips, -1, total.shape[1])
+    got = lax.all_to_all(blocks, ("z", "grp"), 0, 0, tiled=True)
+    return got
+
+
+def arrived(got):
+    return jnp.sum(got.astype(f32), axis=0)
+
+
+def by_strips(
+    frames,
+    grid_size,
+    out_grad,
+    enc_hidden,
+    enc_hidden_m,
+    enc_hidden_v,
+    fore_hidden,
+    fore_hidden_m,
+    fore_hidden_v,
+    enc_input,
+    enc_input_m,
+    enc_input_v,
+    cell_vectors,
+    vectors_m,
+    vectors_v,
+):
+    band = 2 * lax.axis_index("z") + lax.axis_index("core")
+    part = cell_vectors.shape[0]
+    pack = pack_parts(enc_hidden, enc_input, frames[0], cell_vectors.reshape(1, -1))
+    pieces = [pack] + [passed(pack, "z", k) for k in range(1, 4)]
+    cot = out_grad[0].reshape(FRAMES_OUT, 2, 8 * STRIP, HID).transpose(0, 2, 1, 3)
+    first, second = cot_windows(cot)
+    first, *pieces = lax.optimization_barrier((first, *pieces))
+    mine = jnp.concatenate(pieces, axis=0)
+    other = passed(mine, "core", 1)
+    fore_part, mine = lax.optimization_barrier((fore_hidden.astype(bf16), mine))
+    fore_pieces = [fore_part] + [passed(fore_part, "z", k) for k in range(1, 4)]
+    enc_saved, enc_sides, x_own, h3, state, w_enc, weight_xb, vec = forward_enc(grid_size, mine, other)
+    vec_enc, vec_fore = vec[:8], vec[8:]
+    first, h3, *fore_pieces = lax.optimization_barrier((first, h3, *fore_pieces))
+    fore_mine = jnp.concatenate(fore_pieces, axis=0)
+    fore_other = passed(fore_mine, "core", 1)
+    first_got = lax.all_to_all(first, BAND, 0, 0, tiled=True)
+    fore_saved, fore_middle, fore_sides, second, w_fore = forward_fore(
+        grid_size, fore_mine, fore_other, vec_fore, h3, state, second
+    )
+    second_got = lax.all_to_all(second, BAND, 0, 0, tiled=True)
+    og = column_tiles(first_got)
+    d_late, sums, dh, dc, left, right = backward_late(
+        grid_size, w_fore, vec_fore, fore_saved, fore_middle, og
+    )
+    from_left = from_behind(right, BAND, 1)
+    from_right = from_behind(left, BAND, -1)
+    g_late = late_sums(d_late, fore_sides)
+    second_got, from_right = lax.optimization_barrier((second_got, from_right))
+    og_next = second_got.reshape(8, SECOND_COLS, 2, HID)[:, SECOND_PLACE * KEPT :]
+    d_early, sums, dh, dc = backward_early(
+        grid_size,
+        w_fore,
+        vec_fore,
+        fore_saved,
+        og,
+        column_tiles(og_next),
+        (sums, dh, dc, from_left, from_right),
+    )
+    fore_total = chip_sum(*early_sums(d_early, fore_sides, g_late))
+    fore_total, dh = lax.optimization_barrier((fore_total, dh))
+    fore_got = slice_sum(fore_total)
+    d_enc, dx, enc_sums_of = backward_enc(grid_size, w_enc, weight_xb, vec_enc, enc_saved, dh, dc)
+    keep, send = enc_sums(d_enc, enc_sides, x_own, enc_sums_of, sums)
+    fore_got, keep, send, dx, second_got = lax.optimization_barrier((fore_got, keep, send, dx, second_got))
+    enc_sum = chip_sum(keep, send)
+    enc_sum, second_got, dx = lax.optimization_barrier((enc_sum, second_got, dx))
+    enc_got = slice_sum(enc_sum)
+    hidden_block, fore_got = lax.optimization_barrier((join_hidden(second_got), fore_got))
+    input_got = traded(dx.reshape(FRAMES_IN, 8, 2, 256).transpose(1, 0, 2, 3))
+    fore_share = grid_gather(arrived(fore_got).astype(bf16)).astype(f32)
+    enc_total = arrived(enc_got)
+    tail = grid_gather(enc_total.astype(bf16)).astype(f32)
+    enc_share = tail[:, :1152]
+    input_share = tail[:, 1152:1296]
+    vector_share = lax.dynamic_slice_in_dim(enc_total[:, 1296:1408].reshape(-1), band * part, part)
+    return (
+        hidden_block,
+        input_got.transpose(1, 2, 0, 3).reshape(1, FRAMES_IN, 2, -1),
+        *adam_update(enc_hidden, enc_hidden_m, enc_hidden_v, enc_share, matrix_rate),
+        *adam_update(fore_hidden, fore_hidden_m, fore_hidden_v, fore_share, matrix_rate),
+        *adam_update(enc_input, enc_input_m, enc_input_v, input_share, matrix_rate),
+        *adam_update(cell_vectors, vectors_m, vectors_v, vector_share, vector_rate),
+    )
+
+
 def solution(mesh):
-    return jax.shard_map(
-        local,
-        mesh=mesh,
-        in_specs=(
-            P("grp", None, "band", None),
-            P("grp", None),
-            P("grp", None, "band", None),
-            P("band", None),
-            P("band", None),
-            P("band", None),
-            P("band", None),
-            P("band", None),
-            P("band", None),
-            P("band", None),
-            P("band", None),
-            P("band", None),
-            P("band"),
-            P("band"),
-            P("band"),
-        ),
-        out_specs=(
-            P("grp", None, "band", None),
-            P("grp", None, "band", None),
-            P("band", None),
-            P("band", None),
-            P("band", None),
-            P("band", None),
-            P("band", None),
-            P("band", None),
-            P("band", None),
-            P("band", None),
-            P("band", None),
-            P("band", None),
-            P("band", None),
-            P("band", None),
-            P("band"),
-            P("band"),
-            P("band"),
-            P("band"),
-        ),
-        check_vma=False,
-    )
+    groups, bands = mesh.shape["grp"], mesh.shape["band"]
+
+    def run(frames, grid_size, out_grad, *rest):
+        strips = frames.shape[2] == GRID_ROWS and out_grad.shape[3] == STRIP * bands * HID
+        strips = strips and bands == 8 and groups == 4
+        if strips:
+            places = Mesh(mesh.devices.reshape(groups, bands // 2, 2), ("grp", *BAND))
+            body, band = by_strips, BAND
+        else:
+            places, body, band = mesh, by_rows, "band"
+        grid = P("grp", None, band, None)
+        matrix = P(band, None)
+        vector = P(band)
+        return jax.shard_map(
+            body,
+            mesh=places,
+            in_specs=(grid, P("grp", None), grid, *[matrix] * 9, *[vector] * 3),
+            out_specs=(grid, grid, *[matrix] * 12, *[vector] * 4),
+            check_vma=False,
+        )(frames, grid_size, out_grad, *rest)
+
+    return run

time: 841 us -> 215 us (0.26)
  starting transfers between devices: 236 us -> 47.9 us
  other arithmetic: 161 us -> 7.02 us
  matrix products: 143 us -> 0 us
  local copies, waits for them, and re-layouts: 122 us -> 12.5 us
  Pallas kernels: 0 us -> 102 us
  waiting for transfers between devices: 97.8 us -> 43.8 us
  blocking collectives: 50.8 us -> 0 us
  between operations: 14.9 us -> 1.37 us
    ppermute x82 -> x2, starting transfers between devices: 227 us -> 4.31 us  [from_behind(): lax.ppermute(value, axis, [(source, source + steps) for source in range(f...]
    dot_general x100 -> x0, matrix products: 143 us -> none  [the longest x25 70.9 us: weight_grad(): lax.dot_general(gate_grad, patches, (((0,), (0,)), ((), ())), preferred_e...]
    pallas_call x0 -> x11, Pallas kernels: none -> 102 us  [call(): pl.pallas_call(kernel, grid=(grid,), in_specs=[spec(pair) for pair in ins...]
    reduce_sum x62 -> x2, other arithmetic: 45.4 us -> 0.19 us  [arrived(): return jnp.sum(got.astype(f32), axis=0)]
    all_to_all x2 -> x4, waiting for transfers between devices: 55.8 us -> 11.4 us  [the longest x1 5.81 us: by_strips(): second_got = lax.all_to_all(second, BAND, 0, 0, tiled=True)]
    psum x1 -> x0, waiting for transfers between devices: 38.3 us -> none  [local(): lax.psum(shares[0].astype(jnp.bfloat16), 'grp').astype(jnp.float32)]
    while x651 -> x0, local copies, waits for them, and re-layouts: 37.5 us -> none
    concatenate x63 -> x1, other arithmetic: 33.5 us -> 0.08 us  [traded(): both = jnp.concatenate([both, both], axis=0)]
  transfers between devices with their start and end apart: 87 -> 26, of which waited for: 4 -> 13; matrix products, arithmetic and copies ran while one was open for 16% -> 3% of each run, Pallas kernels for 0% -> 40%
where the time goes in v1:
time: 215 us; the launch traced here: 214 us
  Pallas kernels  102 us (47%)
  starting transfers between devices  47.9 us (22%)
  waiting for transfers between devices  43.8 us (20%)
  local copies, waits for them, and re-layouts  12.5 us (6%)
  other arithmetic  7.02 us (3%)
    pallas_call x11, Pallas kernels, call(): pl.pallas_call(kernel, grid=(grid,), in_specs=[spec(pair) for pair in ins...  102 us
    ppermute x20, waiting for transfers between devices, passed(): lax.ppermute(value, axis, [(k, (k + steps) % count) for k in range(count)])  32.4 us
    ppermute x20, starting transfers between devices, passed(): lax.ppermute(value, axis, [(k, (k + steps) % count) for k in range(count)])  26.9 us
    all_to_all x2, starting transfers between devices, slice_sum(): got = lax.all_to_all(blocks, ('z', 'grp'), 0, 0, tiled=True)  9.08 us
    unnamed x92, local copies, waits for them, and re-layouts  7.27 us
    all_to_all x1, waiting for transfers between devices, by_strips(): second_got = lax.all_to_all(second, BAND, 0, 0, tiled=True)  5.81 us
    ppermute x2, starting transfers between devices, from_behind(): lax.ppermute(value, axis, [(source, source + steps) for source in range(f...  4.31 us
  transfers between devices with their start and end apart: 26, of which 13 were waited for; matrix products, arithmetic and copies ran while one was open for 3% of the time, Pallas kernels for 40%

profile of v1, /device:TPU:0, one launch (start us, length us, event | category | flops | bytes accessed | tf_op | source)
XLA Modules:
  0.0 214.4 jit_solution(6813501548542602044)
XLA Ops:
  2.4 3.0 %collective-permute-start = (bf16[80,1408]{1,0:T(8,128)(2,1)}, bf16[80,1408]{1,0:T(8,128)(2,1)S(1)}, u32[]{:S(2)}, u32[]{:S(2)}) collective-permute-start(bf16[80,1408]{1,0:T(8,128)(2,1)} %pack_parts.1), channel_id=1, source_target_pairs={{0,2},{2,4},{4,6},{6,0},{1,3},{3,5},{5,7},{7,1},{8,10},{10,12},{12... | collective-permute-start | bytes 675848 | tf_op jit(solution)/shard_map/ppermute | solution.py:1394
  5.5 2.6 %collective-permute-start.1 = (bf16[80,1408]{1,0:T(8,128)(2,1)}, bf16[80,1408]{1,0:T(8,128)(2,1)S(1)}, u32[]{:S(2)}, u32[]{:S(2)}) collective-permute-start(bf16[80,1408]{1,0:T(8,128)(2,1)} %pack_parts.1), channel_id=1, source_target_pairs={{0,4},{2,6},{4,0},{6,2},{1,5},{3,7},{5,1},{7,3},{8,12},{10,14},{12... | collective-permute-start | bytes 675848 | tf_op jit(solution)/shard_map/ppermute | solution.py:1394
  9.4 3.6 %cot_windows.1 = (bf16[8,390,2,128]{3,2,1,0:T(2,128)(2,1)}, bf16[8,360,2,128]{3,2,1,0:T(2,128)(2,1)}) custom-call(bf16[15,128,2,128]{3,2,1,0:T(2,128)(2,1)} %bitcast.68), custom_call_target="tpu_custom_call" | custom-call | tf_op jit(solution)/shard_map/cot_windows/pallas_call | solution.py:1021
  14.2 8.8 %collective-permute-done.1 = bf16[80,1408]{1,0:T(8,128)(2,1)S(1)} collective-permute-done((bf16[80,1408]{1,0:T(8,128)(2,1)}, bf16[80,1408]{1,0:T(8,128)(2,1)S(1)}, u32[]{:S(2)}, u32[]{:S(2)}) %collective-permute-start.1) | collective-permute-done | bytes 225312 | tf_op jit(solution)/shard_map/ppermute | solution.py:1394
  24.2 5.3 %collective-permute-start.4 = (bf16[64,1152]{1,0:T(8,128)(2,1)S(1)}, bf16[64,1152]{1,0:T(8,128)(2,1)S(1)}, u32[]{:S(2)}, u32[]{:S(2)}) collective-permute-start(bf16[64,1152]{1,0:T(8,128)(2,1)S(1)} %convert_element_type.47), channel_id=1, source_target_pairs={{0,2},{2,4},{4,6},{6,0},{1,3},{3,5},{5,7},{7,1},{8,10},{10,12},{12... | collective-permute-start | bytes 442376 | tf_op jit(solution)/shard_map/ppermute | solution.py:1394
  33.0 16.9 %enc_forward.1 = (f32[5,448,640]{2,1,0:T(8,128)}, bf16[5,288,384]{2,1,0:T(8,128)(2,1)}, bf16[5,256,256]{2,1,0:T(8,128)(2,1)}, bf16[1280,384]{1,0:T(8,128)(2,1)},...) custom-call(s32[1,2]{1,0:T(1,128)} %lim_ref.9, ...), custom_call_target="tpu_custom_call" | custom-call | flops 6794772480 | bytes 10485760 | tf_op jit(solution)/shard_map/enc_forward/pallas_call | solution.py:1021
  49.9 3.8 %all-to-all-start = ((bf16[8,390,2,128]{3,2,1,0:T(2,128)(2,1)}), bf16[8,390,2,128]{3,2,1,0:T(2,128)(2,1)S(1)}, u32[]{:S(2)}, u32[]{:S(2)}) async-start(bf16[8,390,2,128]{3,2,1,0:T(2,128)(2,1)} %get-tuple-element.96), calls=%async_computation | async-start | bytes 3194880 | tf_op jit(solution)/shard_map/all_to_all | solution.py:1471
  56.7 32.5 %fore_forward.1 = (f32[10,576,640]{2,1,0:T(8,128)}, f32[5,416,640]{2,1,0:T(8,128)}, bf16[15,288,384]{2,1,0:T(8,128)(2,1)}, bf16[8,720,128]{2,1,0:T(8,128)(2,1)}, bf16[512,1152]{1,0:T(8,128)(2,1)}) custom-call(s32[1,2]{1,0:T(1,128)} %lim_ref.9, bf16[256,1152]{1,0:T(8,128)(2,1)} %copy-done.26, ...), custom_call_target="tpu_custom_call", output_to_operand_aliasing={{3}: (7, {})} | custom-call | flops 15854469120 | bytes 31457280 | tf_op jit(solution)/shard_map/fore_forward/pallas_call | solution.py:1021
  89.2 2.6 %all-to-all-done = bf16[8,390,2,128]{3,2,1,0:T(2,128)(2,1)S(1)} async-done(((bf16[8,390,2,128]{3,2,1,0:T(2,128)(2,1)}), bf16[8,390,2,128]{3,2,1,0:T(2,128)(2,1)S(1)}, u32[]{:S(2)}, u32[]{:S(2)}) %all-to-all-start) | async-done | bytes 1597472 | tf_op jit(solution)/shard_map/all_to_all | solution.py:1471
  91.8 3.8 %all-to-all-start.1 = ((bf16[8,720,128]{2,1,0:T(8,128)(2,1)}), bf16[8,720,128]{2,1,0:T(8,128)(2,1)S(1)}, u32[]{:S(2)}, u32[]{:S(2)}) async-start(bf16[8,720,128]{2,1,0:T(8,128)(2,1)} %get-tuple-element.97), calls=%async_computation.1 | async-start | bytes 2949120 | tf_op jit(solution)/shard_map/all_to_all | solution.py:1475
  97.8 15.9 %fore_backward_late.1 = (bf16[512,2560]{1,0:T(8,128)(2,1)S(1)}, f32[56,128]{1,0:T(8,128)}, f32[256,128]{1,0:T(8,128)}, f32[256,128]{1,0:T(8,128)}, bf16[2,160,12...) custom-call(s32[1,2]{1,0:T(1,128)} %lim_ref.9, bf16[512,1152]{1,0:T(8,128)(2,1)} %get-tuple-element.94.w_ref, ...), custom_call_target="tpu_custom_call" | custom-call | flops 5662310400 | bytes 20971520 | tf_op jit(solution)/shard_map/fore_backward_late/pallas_call | solution.py:1021
  115.0 3.0 %collective-permute-start.9 = (bf16[2,160,128]{2,1,0:T(8,128)(2,1)}, bf16[2,160,128]{2,1,0:T(8,128)(2,1)S(1)}, u32[]{:S(2)}, u32[]{:S(2)}) collective-permute-start(bf16[2,160,128]{2,1,0:T(8,128)(2,1)} %get-tuple-element.104), channel_id=1, source_target_pairs={{0,1},{1,2},{2,3},{3,4},{4,5},{5,6},{6,7},{8,9},{9,10},{10,11},{11... | collective-permute-start | bytes 245768 | tf_op jit(solution)/shard_map/ppermute | solution.py:29
  120.0 3.7 %late_sums.1.g_in = f32[512,1152]{1,0:T(8,128)S(1)} custom-call(bf16[512,2560]{1,0:T(8,128)(2,1)S(1)} %get-tuple-element.108.dt_ref, bf16[15,288,384]{2,1,0:T(8,128)(2,1)S(1)} %copy-done), custom_call_target="tpu_custom_call" | custom-call | flops 3019898880 | bytes 5000000 | tf_op jit(solution)/shard_map/late_sums/pallas_call | solution.py:1021
  125.2 5.8 %all-to-all-done.1.got_ref = bf16[8,720,128]{2,1,0:T(8,128)(2,1)S(1)} async-done(((bf16[8,720,128]{2,1,0:T(8,128)(2,1)}), bf16[8,720,128]{2,1,0:T(8,128)(2,1)S(1)}, u32[]{:S(2)}, u32[]{:S(2)}) %all-to-all-start.1) | async-done | bytes 1474592 | tf_op jit(solution)/shard_map/all_to_all | solution.py:1475
  132.5 9.7 %fore_backward_early.1 = (bf16[512,1280]{1,0:T(8,128)(2,1)S(1)}, f32[56,128]{1,0:T(8,128)}, f32[576,128]{1,0:T(8,128)}, f32[576,128]{1,0:T(8,128)}) custom-call(s32[1,2]{1,0:T(1,128)S(1)} %copy-done.8, bf16[512,1152]{1,0:T(8,128)(2,1)} %get-tuple-element.94.w_ref, f32[8,128]{1,0:T(8,128)S(1)} %copy-done.6, f32[10,576,640]{2,1,0:T(8,128)} %get-tuple-element.95.sav_ref, ...), custom_call_target="tpu_custom_call" | custom-call | flops 3397386240 | bytes 10485760 | tf_op jit(solution)/shard_map/fore_backward_early/pallas_call | solution.py:1021
  142.2 2.7 %early_sums.1 = (bf16[256,1152]{1,0:T(8,128)(2,1)S(1)}, bf16[256,1152]{1,0:T(8,128)(2,1)S(1)}) custom-call(bf16[512,1280]{1,0:T(8,128)(2,1)S(1)} %get-tuple-element.106.dt_ref, bf16[15,288,384]{2,1,0:T(8,128)(2,1)S(1)} %copy-done.1, f32[512,1152]{1,0:T(8,128)S(1)} %copy-done.3), custom_call_target="tpu_custom_call" | custom-call | flops 1509949440 | bytes 2500000 | tf_op jit(solution)/shard_map/early_sums/pallas_call | solution.py:1021
  147.9 4.6 %all-to-all-start.2 = ((bf16[16,16,1152]{2,1,0:T(8,128)(2,1)}), bf16[16,16,1152]{2,1,0:T(8,128)(2,1)S(1)}, u32[]{:S(2)}, u32[]{:S(2)}) async-start(bf16[16,16,1152]{2,1,0:T(8,128)(2,1)} %bitcast.10), calls=%async_computation.2 | async-start | bytes 1179648 | tf_op jit(solution)/shard_map/all_to_all | solution.py:1430
  152.5 9.0 %enc_backward.1 = (bf16[512,1280]{1,0:T(8,128)(2,1)S(1)}, f32[5,16,256]{2,1,0:T(8,128)}, f32[56,128]{1,0:T(8,128)}) custom-call(s32[1,2]{1,0:T(1,128)} %lim_ref.9, bf16[512,1152]{1,0:T(8,128)(2,1)} %get-tuple-element.113.w_ref, bf16[512,384]{1,0:T(8,128)(2,1)} %get-tuple-element.114.wxb_ref, f32[8,128]{1,0:T(8,128)} %get-tuple-element.159.vec_ref, ...), custom_call_target="tpu_custom_call" | custom-call | flops 2642411520 | bytes 10485760 | tf_op jit(solution)/shard_map/enc_backward/pallas_call | solution.py:1021
  162.3 3.8 %enc_sums.1 = (bf16[256,1408]{1,0:T(8,128)(2,1)S(1)}, bf16[256,1408]{1,0:T(8,128)(2,1)S(1)}) custom-call(bf16[512,1280]{1,0:T(8,128)(2,1)S(1)} %get-tuple-element.118.dt_ref, bf16[5,288,384]{2,1,0:T(8,128)(2,1)S(1)} %copy-done.11, bf16[5,256,256]{2,1,0:T(8,128)(2,1)S(1)} %copy-done.12, bf16[256,256]{1,0:T(8,128)(2,1)S(1)} %copy-done.10, ...), custom_call_target="tpu_custom_call" | custom-call | flops 1509949440 | bytes 2500000 | tf_op jit(solution)/shard_map/enc_sums/pallas_call | solution.py:1021
  166.1 3.0 %all-to-all-done.2 = bf16[16,16,1152]{2,1,0:T(8,128)(2,1)S(1)} async-done(((bf16[16,16,1152]{2,1,0:T(8,128)(2,1)}), bf16[16,16,1152]{2,1,0:T(8,128)(2,1)S(1)}, u32[]{:S(2)}, u32[]{:S(2)}) %all-to-all-start.2) | async-done | bytes 589856 | tf_op jit(solution)/shard_map/all_to_all | solution.py:1430
  179.1 4.5 %all-to-all-start.3 = ((bf16[16,16,1408]{2,1,0:T(8,128)(2,1)}), bf16[16,16,1408]{2,1,0:T(8,128)(2,1)S(1)}, u32[]{:S(2)}, u32[]{:S(2)}) async-start(bf16[16,16,1408]{2,1,0:T(8,128)(2,1)} %bitcast.29), calls=%async_computation.3 | async-start | bytes 1441792 | tf_op jit(solution)/shard_map/all_to_all | solution.py:1430
  185.2 3.8 %collective-permute-start.13 = (f32[2,5,2,256]{3,2,1,0:T(2,128)S(1)}, f32[2,5,2,256]{3,2,1,0:T(2,128)S(1)}, u32[]{:S(2)}, u32[]{:S(2)}) collective-permute-start(f32[2,5,2,256]{3,2,1,0:T(2,128)S(1)} %get-tuple-element.157), channel_id=1, source_target_pairs={{0,6},{2,0},{4,2},{6,4},{1,7},{3,1},{5,3},{7,5},{8,14},{10,8},{12,... | collective-permute-start | bytes 61448 | tf_op jit(solution)/shard_map/ppermute | solution.py:1394
  191.2 4.4 %collective-permute-done.13 = f32[2,5,2,256]{3,2,1,0:T(2,128)S(1)} collective-permute-done((f32[2,5,2,256]{3,2,1,0:T(2,128)S(1)}, f32[2,5,2,256]{3,2,1,0:T(2,128)S(1)}, u32[]{:S(2)}, u32[]{:S(2)}) %collective-permute-start.13) | collective-permute-done | bytes 20512 | tf_op jit(solution)/shard_map/ppermute | solution.py:1394
  195.6 7.9 %collective-permute-done.14 = f32[2,5,2,256]{3,2,1,0:T(2,128)S(1)} collective-permute-done((f32[2,5,2,256]{3,2,1,0:T(2,128)S(1)}, f32[2,5,2,256]{3,2,1,0:T(2,128)S(1)}, u32[]{:S(2)}, u32[]{:S(2)}) %collective-permute-start.14) | collective-permute-done | bytes 20512 | tf_op jit(solution)/shard_map/ppermute | solution.py:1394
  (163 shorter events, 48.4 us)
Async XLA Ops:
  2.4 11.7 %collective-permute-start = (bf16[80,1408]{1,0:T(8,128)(2,1)}, bf16[80,1408]{1,0:T(8,128)(2,1)S(1)}, u32[]{:S(2)}, u32[]{:S(2)}) collective-permute-start(bf16[80,1408]{1,0:T(8,128)(2,1)} %pack_parts.1), channel_id=1, source_target_pairs={{0,2},{2,4},{4,6},{6,0},{1,3},{3,5},{5,7},{7,1},{8,10},{10,12},{12... | collective-permute-start | bytes 675848 | tf_op jit(solution)/shard_map/ppermute | solution.py:1394
  5.5 17.5 %collective-permute-start.1 = (bf16[80,1408]{1,0:T(8,128)(2,1)}, bf16[80,1408]{1,0:T(8,128)(2,1)S(1)}, u32[]{:S(2)}, u32[]{:S(2)}) collective-permute-start(bf16[80,1408]{1,0:T(8,128)(2,1)} %pack_parts.1), channel_id=1, source_target_pairs={{0,4},{2,6},{4,0},{6,2},{1,5},{3,7},{5,1},{7,3},{8,12},{10,14},{12... | collective-permute-start | bytes 675848 | tf_op jit(solution)/shard_map/ppermute | solution.py:1394
  8.1 15.0 %collective-permute-start.2 = (bf16[80,1408]{1,0:T(8,128)(2,1)}, bf16[80,1408]{1,0:T(8,128)(2,1)S(1)}, u32[]{:S(2)}, u32[]{:S(2)}) collective-permute-start(bf16[80,1408]{1,0:T(8,128)(2,1)} %pack_parts.1), channel_id=1, source_target_pairs={{0,6},{2,0},{4,2},{6,4},{1,7},{3,1},{5,3},{7,5},{8,14},{10,8},{12,... | collective-permute-start | bytes 675848 | tf_op jit(solution)/shard_map/ppermute | solution.py:1394
  24.1 7.9 %collective-permute-start.3 = (bf16[320,1408]{1,0:T(8,128)(2,1)S(1)}, bf16[320,1408]{1,0:T(8,128)(2,1)S(1)}, u32[]{:S(2)}, u32[]{:S(2)}) collective-permute-start(bf16[320,1408]{1,0:T(8,128)(2,1)S(1)} %constant_dynamic-update-slice_fusion.mine_ref), channel_id=1, source_target_pairs={{0,1},{1,0},{2,3},{3,2},{4,5},{5,4},{6,7},{7,6},{8,9},{9,8},{10,11... | collective-permute-start | bytes 2703368 | tf_op jit(solution)/shard_map/ppermute | solution.py:1394
  24.2 25.7 %collective-permute-start.4 = (bf16[64,1152]{1,0:T(8,128)(2,1)S(1)}, bf16[64,1152]{1,0:T(8,128)(2,1)S(1)}, u32[]{:S(2)}, u32[]{:S(2)}) collective-permute-start(bf16[64,1152]{1,0:T(8,128)(2,1)S(1)} %convert_element_type.47), channel_id=1, source_target_pairs={{0,2},{2,4},{4,6},{6,0},{1,3},{3,5},{5,7},{7,1},{8,10},{10,12},{12... | collective-permute-start | bytes 442376 | tf_op jit(solution)/shard_map/ppermute | solution.py:1394
  29.5 20.3 %collective-permute-start.5 = (bf16[64,1152]{1,0:T(8,128)(2,1)S(1)}, bf16[64,1152]{1,0:T(8,128)(2,1)S(1)}, u32[]{:S(2)}, u32[]{:S(2)}) collective-permute-start(bf16[64,1152]{1,0:T(8,128)(2,1)S(1)} %convert_element_type.47), channel_id=1, source_target_pairs={{0,4},{2,6},{4,0},{6,2},{1,5},{3,7},{5,1},{7,3},{8,12},{10,14},{12... | collective-permute-start | bytes 442376 | tf_op jit(solution)/shard_map/ppermute | solution.py:1394
  31.1 18.8 %collective-permute-start.6 = (bf16[64,1152]{1,0:T(8,128)(2,1)S(1)}, bf16[64,1152]{1,0:T(8,128)(2,1)S(1)}, u32[]{:S(2)}, u32[]{:S(2)}) collective-permute-start(bf16[64,1152]{1,0:T(8,128)(2,1)S(1)} %convert_element_type.47), channel_id=1, source_target_pairs={{0,6},{2,0},{4,2},{6,4},{1,7},{3,1},{5,3},{7,5},{8,14},{10,8},{12,... | collective-permute-start | bytes 442376 | tf_op jit(solution)/shard_map/ppermute | solution.py:1394
  49.9 41.9 %all-to-all-start = ((bf16[8,390,2,128]{3,2,1,0:T(2,128)(2,1)}), bf16[8,390,2,128]{3,2,1,0:T(2,128)(2,1)S(1)}, u32[]{:S(2)}, u32[]{:S(2)}) async-start(bf16[8,390,2,128]{3,2,1,0:T(2,128)(2,1)} %get-tuple-element.96), calls=%async_computation | async-start | bytes 3194880 | tf_op jit(solution)/shard_map/all_to_all | solution.py:1471
  53.8 2.1 collective-permute-start.7
  91.8 39.2 %all-to-all-start.1 = ((bf16[8,720,128]{2,1,0:T(8,128)(2,1)}), bf16[8,720,128]{2,1,0:T(8,128)(2,1)S(1)}, u32[]{:S(2)}, u32[]{:S(2)}) async-start(bf16[8,720,128]{2,1,0:T(8,128)(2,1)} %get-tuple-element.97), calls=%async_computation.1 | async-start | bytes 2949120 | tf_op jit(solution)/shard_map/all_to_all | solution.py:1475
  113.7 11.5 %collective-permute-start.8 = (bf16[2,160,128]{2,1,0:T(8,128)(2,1)}, bf16[2,160,128]{2,1,0:T(8,128)(2,1)S(1)}, u32[]{:S(2)}, u32[]{:S(2)}) collective-permute-start(bf16[2,160,128]{2,1,0:T(8,128)(2,1)} %get-tuple-element.99), channel_id=1, source_target_pairs={{1,0},{2,1},{3,2},{4,3},{5,4},{6,5},{7,6},{9,8},{10,9},{11,10},{12... | collective-permute-start | bytes 245768 | tf_op jit(solution)/shard_map/ppermute | solution.py:29
  115.0 17.4 %collective-permute-start.9 = (bf16[2,160,128]{2,1,0:T(8,128)(2,1)}, bf16[2,160,128]{2,1,0:T(8,128)(2,1)S(1)}, u32[]{:S(2)}, u32[]{:S(2)}) collective-permute-start(bf16[2,160,128]{2,1,0:T(8,128)(2,1)} %get-tuple-element.104), channel_id=1, source_target_pairs={{0,1},{1,2},{2,3},{3,4},{4,5},{5,6},{6,7},{8,9},{9,10},{10,11},{11... | collective-permute-start | bytes 245768 | tf_op jit(solution)/shard_map/ppermute | solution.py:29
  147.9 21.1 %all-to-all-start.2 = ((bf16[16,16,1152]{2,1,0:T(8,128)(2,1)}), bf16[16,16,1152]{2,1,0:T(8,128)(2,1)S(1)}, u32[]{:S(2)}, u32[]{:S(2)}) async-start(bf16[16,16,1152]{2,1,0:T(8,128)(2,1)} %bitcast.10), calls=%async_computation.2 | async-start | bytes 1179648 | tf_op jit(solution)/shard_map/all_to_all | solution.py:1430
  169.0 2.3 %collective-permute-start.11 = (bf16[256,1408]{1,0:T(8,128)(2,1)S(1)}, bf16[256,1408]{1,0:T(8,128)(2,1)}, u32[]{:S(2)}, u32[]{:S(2)}) collective-permute-start(bf16[256,1408]{1,0:T(8,128)(2,1)S(1)} %get-tuple-element.127), channel_id=1, source_target_pairs={{0,1},{1,0},{2,3},{3,2},{4,5},{5,4},{6,7},{7,6},{8,9},{9,8},{10,11... | collective-permute-start | bytes 2162696 | tf_op jit(solution)/shard_map/ppermute | solution.py:1394
  175.9 7.9 %collective-permute-start.19 = (bf16[16,1152]{1,0:T(8,128)(2,1)S(1)}, bf16[16,1152]{1,0:T(8,128)(2,1)S(1)}, u32[]{:S(2)}, u32[]{:S(2)}) collective-permute-start(bf16[16,1152]{1,0:T(8,128)(2,1)S(1)} %reduce_sum.22), channel_id=1, source_target_pairs={{0,24},{8,0},{16,8},{24,16},{1,25},{9,1},{17,9},{25,17},{2,26},{10... | collective-permute-start | bytes 110600 | tf_op jit(solution)/shard_map/ppermute | solution.py:1394
  177.1 6.8 %collective-permute-start.20 = (bf16[16,1152]{1,0:T(8,128)(2,1)S(1)}, bf16[16,1152]{1,0:T(8,128)(2,1)S(1)}, u32[]{:S(2)}, u32[]{:S(2)}) collective-permute-start(bf16[16,1152]{1,0:T(8,128)(2,1)S(1)} %reduce_sum.22), channel_id=1, source_target_pairs={{0,16},{8,24},{16,0},{24,8},{1,17},{9,25},{17,1},{25,9},{2,18},{10... | collective-permute-start | bytes 110600 | tf_op jit(solution)/shard_map/ppermute | solution.py:1394
  177.9 5.9 %collective-permute-start.21 = (bf16[16,1152]{1,0:T(8,128)(2,1)S(1)}, bf16[16,1152]{1,0:T(8,128)(2,1)S(1)}, u32[]{:S(2)}, u32[]{:S(2)}) collective-permute-start(bf16[16,1152]{1,0:T(8,128)(2,1)S(1)} %reduce_sum.22), channel_id=1, source_target_pairs={{0,8},{8,16},{16,24},{24,0},{1,9},{9,17},{17,25},{25,1},{2,10},{10... | collective-permute-start | bytes 110600 | tf_op jit(solution)/shard_map/ppermute | solution.py:1394
  179.1 25.3 %all-to-all-start.3 = ((bf16[16,16,1408]{2,1,0:T(8,128)(2,1)}), bf16[16,16,1408]{2,1,0:T(8,128)(2,1)S(1)}, u32[]{:S(2)}, u32[]{:S(2)}) async-start(bf16[16,16,1408]{2,1,0:T(8,128)(2,1)} %bitcast.29), calls=%async_computation.3 | async-start | bytes 1441792 | tf_op jit(solution)/shard_map/all_to_all | solution.py:1430
  185.2 10.5 %collective-permute-start.13 = (f32[2,5,2,256]{3,2,1,0:T(2,128)S(1)}, f32[2,5,2,256]{3,2,1,0:T(2,128)S(1)}, u32[]{:S(2)}, u32[]{:S(2)}) collective-permute-start(f32[2,5,2,256]{3,2,1,0:T(2,128)S(1)} %get-tuple-element.157), channel_id=1, source_target_pairs={{0,6},{2,0},{4,2},{6,4},{1,7},{3,1},{5,3},{7,5},{8,14},{10,8},{12,... | collective-permute-start | bytes 61448 | tf_op jit(solution)/shard_map/ppermute | solution.py:1394
  190.0 13.5 %collective-permute-start.14 = (f32[2,5,2,256]{3,2,1,0:T(2,128)S(1)}, f32[2,5,2,256]{3,2,1,0:T(2,128)S(1)}, u32[]{:S(2)}, u32[]{:S(2)}) collective-permute-start(f32[2,5,2,256]{3,2,1,0:T(2,128)S(1)} %get-tuple-element.158), channel_id=1, source_target_pairs={{0,4},{2,6},{4,0},{6,2},{1,5},{3,7},{5,1},{7,3},{8,12},{10,14},{12... | collective-permute-start | bytes 61448 | tf_op jit(solution)/shard_map/ppermute | solution.py:1394
  190.1 13.4 %collective-permute-start.15 = (f32[2,5,2,256]{3,2,1,0:T(2,128)S(1)}, f32[2,5,2,256]{3,2,1,0:T(2,128)S(1)}, u32[]{:S(2)}, u32[]{:S(2)}) collective-permute-start(f32[2,5,2,256]{3,2,1,0:T(2,128)S(1)} %get-tuple-element.156), channel_id=1, source_target_pairs={{0,2},{2,4},{4,6},{6,0},{1,3},{3,5},{5,7},{7,1},{8,10},{10,12},{12... | collective-permute-start | bytes 61448 | tf_op jit(solution)/shard_map/ppermute | solution.py:1394
  204.5 4.4 %collective-permute-start.16 = (bf16[16,1408]{1,0:T(8,128)(2,1)S(1)}, bf16[16,1408]{1,0:T(8,128)(2,1)S(1)}, u32[]{:S(2)}, u32[]{:S(2)}) collective-permute-start(bf16[16,1408]{1,0:T(8,128)(2,1)S(1)} %get-tuple-element.153), channel_id=1, source_target_pairs={{0,24},{8,0},{16,8},{24,16},{1,25},{9,1},{17,9},{25,17},{2,26},{10... | collective-permute-start | bytes 135176 | tf_op jit(solution)/shard_map/ppermute | solution.py:1394
  206.9 4.0 %collective-permute-start.17 = (bf16[16,1408]{1,0:T(8,128)(2,1)S(1)}, bf16[16,1408]{1,0:T(8,128)(2,1)S(1)}, u32[]{:S(2)}, u32[]{:S(2)}) collective-permute-start(bf16[16,1408]{1,0:T(8,128)(2,1)S(1)} %get-tuple-element.153), channel_id=1, source_target_pairs={{0,16},{8,24},{16,0},{24,8},{1,17},{9,25},{17,1},{25,9},{2,18},{10... | collective-permute-start | bytes 135176 | tf_op jit(solution)/shard_map/ppermute | solution.py:1394
  207.5 4.9 %collective-permute-start.18 = (bf16[16,1408]{1,0:T(8,128)(2,1)S(1)}, bf16[16,1408]{1,0:T(8,128)(2,1)S(1)}, u32[]{:S(2)}, u32[]{:S(2)}) collective-permute-start(bf16[16,1408]{1,0:T(8,128)(2,1)S(1)} %get-tuple-element.153), channel_id=1, source_target_pairs={{0,8},{8,16},{16,24},{24,0},{1,9},{9,17},{17,25},{25,1},{2,10},{10... | collective-permute-start | bytes 135176 | tf_op jit(solution)/shard_map/ppermute | solution.py:1394
  (35 other events, 269.2 us)

commit v2 on v1

--- a/solution.py
+++ b/solution.py
@@ -362,11 +362,14 @@
 
 
 def row_moves(value):
-    total = value.shape[0]
-    row = lax.broadcasted_iota(jnp.int32, value.shape, 0) & (GRID_ROWS - 1)
-    above = jnp.where(row == 0, 0.0, pltpu.roll(value, 1, 0))
-    below = jnp.where(row == GRID_ROWS - 1, 0.0, pltpu.roll(value, total - 1, 0))
-    return above, below
+    halves = value.reshape(-1, 2, 8, HID)
+    first, second = halves[:, 0], halves[:, 1]
+    row = lax.broadcasted_iota(jnp.int32, first.shape, 1)
+    first_down, second_down = pltpu.roll(first, 1, 1), pltpu.roll(second, 1, 1)
+    first_up, second_up = pltpu.roll(first, 7, 1), pltpu.roll(second, 7, 1)
+    above = [jnp.where(row == 0, 0.0, first_down), jnp.where(row == 0, first_down, second_down)]
+    below = [jnp.where(row == 7, second_up, first_up), jnp.where(row == 7, 0.0, second_up)]
+    return tuple(jnp.stack(pair, axis=1).reshape(value.shape) for pair in (above, below))
 
 
 def own_column():
@@ -431,7 +434,7 @@
     vec = [vec_ref[k : k + 1, :] for k in range(7)]
 
     def cell_of(col, count):
-        for piece in cuts(col, col + count, 4, (kept, last)):
+        for piece in cuts(col, col + count, 8, (kept, last)):
             cell_piece(z_ref, next_ref, c_ref, mask_ref, vec, sav_ref, lo, *piece, kept, last)
 
     waiting = None
@@ -511,7 +514,7 @@
         copy_windows(cot_ref, 2 * FRAMES_IN + k, first_ref, KEPT * (2 + k), REACH)
         copy_windows(cot_ref, FRAMES_IN + k, first_ref, MID_COLS * (MID_PLACE + k), REACH_MID)
     for k in range(3):
-        copy_windows(cot_ref, 2 - k, second_ref, KEPT * (SECOND_PLACE + k), REACH)
+        copy_windows(cot_ref, 2 - k, second_ref, SECOND_PLACE + KEPT * k, REACH)
 
 
 def fill_frames(lim_ref, mine_ref, other_ref, line_ref, vec_ref, wide_ref, pairs_ref, pair_ref):
@@ -540,10 +543,12 @@
         for band in range(8):
             line_ref[frame, 1, 2 * band : 2 * band + 2, :] = wide_ref[band, frame, :, pl.ds(start, lanes)]
         field = jnp.where(inside, line_ref[frame, 1], 0.0)
-        above, below = row_moves(field)
-        line_ref[frame, 0] = above
         line_ref[frame, 1] = field
-        line_ref[frame, 2] = below
+        for block in range(FRAME_COLS // 8):
+            part = slice(HID * block, HID * (block + 1))
+            above, below = row_moves(line_ref[frame, 1, :, part])
+            line_ref[frame, 0, :, part] = above
+            line_ref[frame, 2, :, part] = below
     lane = lax.broadcasted_iota(jnp.int32, (1, HID), 1)
     for k in range(14):
         at, offset = divmod(HID * k, 112)
@@ -781,7 +786,7 @@
     done = lo
     for k, (col, count) in enumerate(pieces):
         last = min(col + count + 1, hi)
-        for place, width in cuts(done, last, 4, (own, own + STRIP)):
+        for place, width in cuts(done, last, 8, (own, own + STRIP)):
             back_piece(refs, vec, place, width, own <= place < own + STRIP, kept)
         done = last
         if k > 0:
@@ -1004,9 +1009,9 @@
 MID_COLS = STRIP + 2 * REACH_MID
 MID_CELLS = MID_COLS * GRID_ROWS
 MID_PLACE = 10
-SECOND_PLACE = 7
+SECOND_PLACE = FRAMES_OUT * STRIP
 FIRST_COLS = MID_COLS * (MID_PLACE + FRAMES_IN)
-SECOND_COLS = KEPT * (SECOND_PLACE + 3)
+SECOND_COLS = SECOND_PLACE + 3 * KEPT
 
 
 def held(shape, dtype):
@@ -1481,7 +1486,7 @@
     from_right = from_behind(left, BAND, -1)
     g_late = late_sums(d_late, fore_sides)
     second_got, from_right = lax.optimization_barrier((second_got, from_right))
-    og_next = second_got.reshape(8, SECOND_COLS, 2, HID)[:, SECOND_PLACE * KEPT :]
+    og_next = second_got.reshape(8, SECOND_COLS, 2, HID)[:, SECOND_PLACE:]
     d_early, sums, dh, dc = backward_early(
         grid_size,
         w_fore,
@@ -1498,18 +1503,18 @@
     keep, send = enc_sums(d_enc, enc_sides, x_own, enc_sums_of, sums)
     fore_got, keep, send, dx, second_got = lax.optimization_barrier((fore_got, keep, send, dx, second_got))
     enc_sum = chip_sum(keep, send)
-    enc_sum, second_got, dx = lax.optimization_barrier((enc_sum, second_got, dx))
+    enc_sum, second_got, dx, fore_got = lax.optimization_barrier((enc_sum, second_got, dx, fore_got))
     enc_got = slice_sum(enc_sum)
-    hidden_block, fore_got = lax.optimization_barrier((join_hidden(second_got), fore_got))
     input_got = traded(dx.reshape(FRAMES_IN, 8, 2, 256).transpose(1, 0, 2, 3))
-    fore_share = grid_gather(arrived(fore_got).astype(bf16)).astype(f32)
+    fore_sum = arrived(fore_got)
     enc_total = arrived(enc_got)
-    tail = grid_gather(enc_total.astype(bf16)).astype(f32)
+    tail = grid_gather(jnp.concatenate([enc_total, fore_sum], axis=1).astype(bf16)).astype(f32)
     enc_share = tail[:, :1152]
     input_share = tail[:, 1152:1296]
+    fore_share = tail[:, 1408:]
     vector_share = lax.dynamic_slice_in_dim(enc_total[:, 1296:1408].reshape(-1), band * part, part)
     return (
-        hidden_block,
+        join_hidden(second_got),
         input_got.transpose(1, 2, 0, 3).reshape(1, FRAMES_IN, 2, -1),
         *adam_update(enc_hidden, enc_hidden_m, enc_hidden_v, enc_share, matrix_rate),
         *adam_update(fore_hidden, fore_hidden_m, fore_hidden_v, fore_share, matrix_rate),

time: 215 us -> 212 us (0.986)
  starting transfers between devices: 47.9 us -> 45.1 us
    ppermute x20 -> x17, starting transfers between devices: 26.9 us -> 25 us  [passed(): lax.ppermute(value, axis, [(k, (k + steps) % count) for k in range(count)])]
    ppermute x20 -> x17, waiting for transfers between devices: 32.4 us -> 34.1 us  [passed(): lax.ppermute(value, axis, [(k, (k + steps) % count) for k in range(count)])]
    unnamed x92 -> x84, local copies, waits for them, and re-layouts: 7.27 us -> 7.18 us
  transfers between devices with their start and end apart: 26 -> 23, of which waited for: 13 -> 13; matrix products, arithmetic and copies ran while one was open for 3% -> 3% of each run, Pallas kernels for 40% -> 41%
where the time goes in v2:
time: 212 us; the launch traced here: 211 us
  Pallas kernels  102 us (48%)
  starting transfers between devices  45.1 us (21%)
  waiting for transfers between devices  44.5 us (21%)
  local copies, waits for them, and re-layouts  12.4 us (6%)
  other arithmetic  6.31 us (3%)
    pallas_call x11, Pallas kernels, call(): pl.pallas_call(kernel, grid=(grid,), in_specs=[spec(pair) for pair in ins...  102 us
    ppermute x17, waiting for transfers between devices, passed(): lax.ppermute(value, axis, [(k, (k + steps) % count) for k in range(count)])  34.1 us
    ppermute x17, starting transfers between devices, passed(): lax.ppermute(value, axis, [(k, (k + steps) % count) for k in range(count)])  25 us
    all_to_all x2, starting transfers between devices, slice_sum(): got = lax.all_to_all(blocks, ('z', 'grp'), 0, 0, tiled=True)  8.16 us
    unnamed x84, local copies, waits for them, and re-layouts  7.18 us
    all_to_all x1, waiting for transfers between devices, by_strips(): second_got = lax.all_to_all(second, BAND, 0, 0, tiled=True)  4.79 us
    ppermute x2, starting transfers between devices, from_behind(): lax.ppermute(value, axis, [(source, source + steps) for source in range(f...  4.31 us
  transfers between devices with their start and end apart: 23, of which 13 were waited for; matrix products, arithmetic and copies ran while one was open for 3% of the time, Pallas kernels for 41%

profile of v2, /device:TPU:0, one launch (start us, length us, event | category | flops | bytes accessed | tf_op | source)
XLA Modules:
  0.0 211.3 jit_solution(11049574234055510520)
XLA Ops:
  2.4 3.0 %collective-permute-start = (bf16[80,1408]{1,0:T(8,128)(2,1)}, bf16[80,1408]{1,0:T(8,128)(2,1)S(1)}, u32[]{:S(2)}, u32[]{:S(2)}) collective-permute-start(bf16[80,1408]{1,0:T(8,128)(2,1)} %pack_parts.1), channel_id=1, source_target_pairs={{0,2},{2,4},{4,6},{6,0},{1,3},{3,5},{5,7},{7,1},{8,10},{10,12},{12... | collective-permute-start | bytes 675848 | tf_op jit(solution)/shard_map/ppermute | solution.py:1399
  5.5 2.6 %collective-permute-start.1 = (bf16[80,1408]{1,0:T(8,128)(2,1)}, bf16[80,1408]{1,0:T(8,128)(2,1)S(1)}, u32[]{:S(2)}, u32[]{:S(2)}) collective-permute-start(bf16[80,1408]{1,0:T(8,128)(2,1)} %pack_parts.1), channel_id=1, source_target_pairs={{0,4},{2,6},{4,0},{6,2},{1,5},{3,7},{5,1},{7,3},{8,12},{10,14},{12... | collective-permute-start | bytes 675848 | tf_op jit(solution)/shard_map/ppermute | solution.py:1399
  9.4 3.6 %cot_windows.1 = (bf16[8,390,2,128]{3,2,1,0:T(2,128)(2,1)}, bf16[8,348,2,128]{3,2,1,0:T(2,128)(2,1)}) custom-call(bf16[15,128,2,128]{3,2,1,0:T(2,128)(2,1)} %bitcast.69), custom_call_target="tpu_custom_call" | custom-call | tf_op jit(solution)/shard_map/cot_windows/pallas_call | solution.py:1026
  14.2 8.8 %collective-permute-done.1 = bf16[80,1408]{1,0:T(8,128)(2,1)S(1)} collective-permute-done((bf16[80,1408]{1,0:T(8,128)(2,1)}, bf16[80,1408]{1,0:T(8,128)(2,1)S(1)}, u32[]{:S(2)}, u32[]{:S(2)}) %collective-permute-start.1) | collective-permute-done | bytes 225312 | tf_op jit(solution)/shard_map/ppermute | solution.py:1399
  24.2 5.3 %collective-permute-start.4 = (bf16[64,1152]{1,0:T(8,128)(2,1)S(1)}, bf16[64,1152]{1,0:T(8,128)(2,1)S(1)}, u32[]{:S(2)}, u32[]{:S(2)}) collective-permute-start(bf16[64,1152]{1,0:T(8,128)(2,1)S(1)} %convert_element_type.43), channel_id=1, source_target_pairs={{0,2},{2,4},{4,6},{6,0},{1,3},{3,5},{5,7},{7,1},{8,10},{10,12},{12... | collective-permute-start | bytes 442376 | tf_op jit(solution)/shard_map/ppermute | solution.py:1399
  32.9 17.0 %enc_forward.1 = (f32[5,448,640]{2,1,0:T(8,128)}, bf16[5,288,384]{2,1,0:T(8,128)(2,1)}, bf16[5,256,256]{2,1,0:T(8,128)(2,1)}, bf16[1280,384]{1,0:T(8,128)(2,1)},...) custom-call(s32[1,2]{1,0:T(1,128)} %lim_ref.9, ...), custom_call_target="tpu_custom_call" | custom-call | flops 6794772480 | bytes 10485760 | tf_op jit(solution)/shard_map/enc_forward/pallas_call | solution.py:1026
  50.0 3.8 %all-to-all-start = ((bf16[8,390,2,128]{3,2,1,0:T(2,128)(2,1)}), bf16[8,390,2,128]{3,2,1,0:T(2,128)(2,1)S(1)}, u32[]{:S(2)}, u32[]{:S(2)}) async-start(bf16[8,390,2,128]{3,2,1,0:T(2,128)(2,1)} %get-tuple-element.95), calls=%async_computation | async-start | bytes 3194880 | tf_op jit(solution)/shard_map/all_to_all | solution.py:1476
  56.7 32.4 %fore_forward.1 = (f32[10,576,640]{2,1,0:T(8,128)}, f32[5,416,640]{2,1,0:T(8,128)}, bf16[15,288,384]{2,1,0:T(8,128)(2,1)}, bf16[8,696,128]{2,1,0:T(8,128)(2,1)}, bf16[512,1152]{1,0:T(8,128)(2,1)}) custom-call(s32[1,2]{1,0:T(1,128)} %lim_ref.9, bf16[256,1152]{1,0:T(8,128)(2,1)} %copy-done.26, ...), custom_call_target="tpu_custom_call", output_to_operand_aliasing={{3}: (7, {})} | custom-call | flops 15854469120 | bytes 31457280 | tf_op jit(solution)/shard_map/fore_forward/pallas_call | solution.py:1026
  89.2 2.7 %all-to-all-done = bf16[8,390,2,128]{3,2,1,0:T(2,128)(2,1)S(1)} async-done(((bf16[8,390,2,128]{3,2,1,0:T(2,128)(2,1)}), bf16[8,390,2,128]{3,2,1,0:T(2,128)(2,1)S(1)}, u32[]{:S(2)}, u32[]{:S(2)}) %all-to-all-start) | async-done | bytes 1597472 | tf_op jit(solution)/shard_map/all_to_all | solution.py:1476
  91.8 3.8 %all-to-all-start.1 = ((bf16[8,696,128]{2,1,0:T(8,128)(2,1)}), bf16[8,696,128]{2,1,0:T(8,128)(2,1)S(1)}, u32[]{:S(2)}, u32[]{:S(2)}) async-start(bf16[8,696,128]{2,1,0:T(8,128)(2,1)} %get-tuple-element.96), calls=%async_computation.1 | async-start | bytes 2850816 | tf_op jit(solution)/shard_map/all_to_all | solution.py:1480
  97.9 15.8 %fore_backward_late.1 = (bf16[512,2560]{1,0:T(8,128)(2,1)S(1)}, f32[56,128]{1,0:T(8,128)}, f32[256,128]{1,0:T(8,128)}, f32[256,128]{1,0:T(8,128)}, bf16[2,160,12...) custom-call(s32[1,2]{1,0:T(1,128)} %lim_ref.9, bf16[512,1152]{1,0:T(8,128)(2,1)} %get-tuple-element.93.w_ref, ...), custom_call_target="tpu_custom_call" | custom-call | flops 5662310400 | bytes 20971520 | tf_op jit(solution)/shard_map/fore_backward_late/pallas_call | solution.py:1026
  115.0 3.0 %collective-permute-start.9 = (bf16[2,160,128]{2,1,0:T(8,128)(2,1)}, bf16[2,160,128]{2,1,0:T(8,128)(2,1)S(1)}, u32[]{:S(2)}, u32[]{:S(2)}) collective-permute-start(bf16[2,160,128]{2,1,0:T(8,128)(2,1)} %get-tuple-element.103), channel_id=1, source_target_pairs={{0,1},{1,2},{2,3},{3,4},{4,5},{5,6},{6,7},{8,9},{9,10},{10,11},{11... | collective-permute-start | bytes 245768 | tf_op jit(solution)/shard_map/ppermute | solution.py:29
  120.0 3.7 %late_sums.1.g_in = f32[512,1152]{1,0:T(8,128)S(1)} custom-call(bf16[512,2560]{1,0:T(8,128)(2,1)S(1)} %get-tuple-element.107.dt_ref, bf16[15,288,384]{2,1,0:T(8,128)(2,1)S(1)} %copy-done), custom_call_target="tpu_custom_call" | custom-call | flops 3019898880 | bytes 5000000 | tf_op jit(solution)/shard_map/late_sums/pallas_call | solution.py:1026
  125.2 4.8 %all-to-all-done.1.got_ref = bf16[8,696,128]{2,1,0:T(8,128)(2,1)S(1)} async-done(((bf16[8,696,128]{2,1,0:T(8,128)(2,1)}), bf16[8,696,128]{2,1,0:T(8,128)(2,1)S(1)}, u32[]{:S(2)}, u32[]{:S(2)}) %all-to-all-start.1) | async-done | bytes 1425440 | tf_op jit(solution)/shard_map/all_to_all | solution.py:1480
  131.5 9.7 %fore_backward_early.1 = (bf16[512,1280]{1,0:T(8,128)(2,1)S(1)}, f32[56,128]{1,0:T(8,128)}, f32[576,128]{1,0:T(8,128)}, f32[576,128]{1,0:T(8,128)}) custom-call(s32[1,2]{1,0:T(1,128)S(1)} %copy-done.8, bf16[512,1152]{1,0:T(8,128)(2,1)} %get-tuple-element.93.w_ref, f32[8,128]{1,0:T(8,128)S(1)} %copy-done.6, f32[10,576,640]{2,1,0:T(8,128)} %get-tuple-element.94.sav_ref, ...), custom_call_target="tpu_custom_call" | custom-call | flops 3397386240 | bytes 10485760 | tf_op jit(solution)/shard_map/fore_backward_early/pallas_call | solution.py:1026
  141.2 2.7 %early_sums.1 = (bf16[256,1152]{1,0:T(8,128)(2,1)S(1)}, bf16[256,1152]{1,0:T(8,128)(2,1)S(1)}) custom-call(bf16[512,1280]{1,0:T(8,128)(2,1)S(1)} %get-tuple-element.105.dt_ref, bf16[15,288,384]{2,1,0:T(8,128)(2,1)S(1)} %copy-done.1, f32[512,1152]{1,0:T(8,128)S(1)} %copy-done.3), custom_call_target="tpu_custom_call" | custom-call | flops 1509949440 | bytes 2500000 | tf_op jit(solution)/shard_map/early_sums/pallas_call | solution.py:1026
  146.9 4.6 %all-to-all-start.2 = ((bf16[16,16,1152]{2,1,0:T(8,128)(2,1)}), bf16[16,16,1152]{2,1,0:T(8,128)(2,1)S(1)}, u32[]{:S(2)}, u32[]{:S(2)}) async-start(bf16[16,16,1152]{2,1,0:T(8,128)(2,1)} %bitcast.10), calls=%async_computation.2 | async-start | bytes 1179648 | tf_op jit(solution)/shard_map/all_to_all | solution.py:1435
  151.5 9.0 %enc_backward.1 = (bf16[512,1280]{1,0:T(8,128)(2,1)S(1)}, f32[5,16,256]{2,1,0:T(8,128)}, f32[56,128]{1,0:T(8,128)}) custom-call(s32[1,2]{1,0:T(1,128)} %lim_ref.9, bf16[512,1152]{1,0:T(8,128)(2,1)} %get-tuple-element.112.w_ref, bf16[512,384]{1,0:T(8,128)(2,1)} %get-tuple-element.113.wxb_ref, f32[8,128]{1,0:T(8,128)} %get-tuple-element.161.vec_ref, ...), custom_call_target="tpu_custom_call" | custom-call | flops 2642411520 | bytes 10485760 | tf_op jit(solution)/shard_map/enc_backward/pallas_call | solution.py:1026
  161.2 3.8 %enc_sums.1 = (bf16[256,1408]{1,0:T(8,128)(2,1)S(1)}, bf16[256,1408]{1,0:T(8,128)(2,1)S(1)}) custom-call(bf16[512,1280]{1,0:T(8,128)(2,1)S(1)} %get-tuple-element.117.dt_ref, bf16[5,288,384]{2,1,0:T(8,128)(2,1)S(1)} %copy-done.11, bf16[5,256,256]{2,1,0:T(8,128)(2,1)S(1)} %copy-done.12, bf16[256,256]{1,0:T(8,128)(2,1)S(1)} %copy-done.10, ...), custom_call_target="tpu_custom_call" | custom-call | flops 1509949440 | bytes 2500000 | tf_op jit(solution)/shard_map/enc_sums/pallas_call | solution.py:1026
  165.0 2.9 %all-to-all-done.2 = bf16[16,16,1152]{2,1,0:T(8,128)(2,1)S(1)} async-done(((bf16[16,16,1152]{2,1,0:T(8,128)(2,1)}), bf16[16,16,1152]{2,1,0:T(8,128)(2,1)S(1)}, u32[]{:S(2)}, u32[]{:S(2)}) %all-to-all-start.2) | async-done | bytes 589856 | tf_op jit(solution)/shard_map/all_to_all | solution.py:1435
  175.8 3.6 %all-to-all-start.3 = ((bf16[16,16,1408]{2,1,0:T(8,128)(2,1)}), bf16[16,16,1408]{2,1,0:T(8,128)(2,1)S(1)}, u32[]{:S(2)}, u32[]{:S(2)}) async-start(bf16[16,16,1408]{2,1,0:T(8,128)(2,1)} %bitcast.29), calls=%async_computation.3 | async-start | bytes 1441792 | tf_op jit(solution)/shard_map/all_to_all | solution.py:1435
  181.7 2.8 %collective-permute-start.14 = (f32[2,5,2,256]{3,2,1,0:T(2,128)S(1)}, f32[2,5,2,256]{3,2,1,0:T(2,128)S(1)}, u32[]{:S(2)}, u32[]{:S(2)}) collective-permute-start(f32[2,5,2,256]{3,2,1,0:T(2,128)S(1)} %get-tuple-element.160), channel_id=1, source_target_pairs={{0,4},{2,6},{4,0},{6,2},{1,5},{3,7},{5,1},{7,3},{8,12},{10,14},{12... | collective-permute-start | bytes 61448 | tf_op jit(solution)/shard_map/ppermute | solution.py:1399
  186.1 13.5 %collective-permute-done.14 = f32[2,5,2,256]{3,2,1,0:T(2,128)S(1)} collective-permute-done((f32[2,5,2,256]{3,2,1,0:T(2,128)S(1)}, f32[2,5,2,256]{3,2,1,0:T(2,128)S(1)}, u32[]{:S(2)}, u32[]{:S(2)}) %collective-permute-start.14) | collective-permute-done | bytes 20512 | tf_op jit(solution)/shard_map/ppermute | solution.py:1399
  205.2 2.6 %collective-permute-done.17 = bf16[16,2560]{1,0:T(8,128)(2,1)S(1)} collective-permute-done((bf16[16,2560]{1,0:T(8,128)(2,1)S(1)}, bf16[16,2560]{1,0:T(8,128)(2,1)S(1)}, u32[]{:S(2)}, u32[]{:S(2)}) %collective-permute-start.17) | collective-permute-done | bytes 81952 | tf_op jit(solution)/shard_map/ppermute | solution.py:1399
  (149 shorter events, 44.5 us)
Async XLA Ops:
  2.4 11.7 %collective-permute-start = (bf16[80,1408]{1,0:T(8,128)(2,1)}, bf16[80,1408]{1,0:T(8,128)(2,1)S(1)}, u32[]{:S(2)}, u32[]{:S(2)}) collective-permute-start(bf16[80,1408]{1,0:T(8,128)(2,1)} %pack_parts.1), channel_id=1, source_target_pairs={{0,2},{2,4},{4,6},{6,0},{1,3},{3,5},{5,7},{7,1},{8,10},{10,12},{12... | collective-permute-start | bytes 675848 | tf_op jit(solution)/shard_map/ppermute | solution.py:1399
  5.5 17.5 %collective-permute-start.1 = (bf16[80,1408]{1,0:T(8,128)(2,1)}, bf16[80,1408]{1,0:T(8,128)(2,1)S(1)}, u32[]{:S(2)}, u32[]{:S(2)}) collective-permute-start(bf16[80,1408]{1,0:T(8,128)(2,1)} %pack_parts.1), channel_id=1, source_target_pairs={{0,4},{2,6},{4,0},{6,2},{1,5},{3,7},{5,1},{7,3},{8,12},{10,14},{12... | collective-permute-start | bytes 675848 | tf_op jit(solution)/shard_map/ppermute | solution.py:1399
  8.1 15.0 %collective-permute-start.2 = (bf16[80,1408]{1,0:T(8,128)(2,1)}, bf16[80,1408]{1,0:T(8,128)(2,1)S(1)}, u32[]{:S(2)}, u32[]{:S(2)}) collective-permute-start(bf16[80,1408]{1,0:T(8,128)(2,1)} %pack_parts.1), channel_id=1, source_target_pairs={{0,6},{2,0},{4,2},{6,4},{1,7},{3,1},{5,3},{7,5},{8,14},{10,8},{12,... | collective-permute-start | bytes 675848 | tf_op jit(solution)/shard_map/ppermute | solution.py:1399
  24.1 7.9 %collective-permute-start.3 = (bf16[320,1408]{1,0:T(8,128)(2,1)S(1)}, bf16[320,1408]{1,0:T(8,128)(2,1)S(1)}, u32[]{:S(2)}, u32[]{:S(2)}) collective-permute-start(bf16[320,1408]{1,0:T(8,128)(2,1)S(1)} %constant_dynamic-update-slice_fusion.mine_ref), channel_id=1, source_target_pairs={{0,1},{1,0},{2,3},{3,2},{4,5},{5,4},{6,7},{7,6},{8,9},{9,8},{10,11... | collective-permute-start | bytes 2703368 | tf_op jit(solution)/shard_map/ppermute | solution.py:1399
  24.2 25.7 %collective-permute-start.4 = (bf16[64,1152]{1,0:T(8,128)(2,1)S(1)}, bf16[64,1152]{1,0:T(8,128)(2,1)S(1)}, u32[]{:S(2)}, u32[]{:S(2)}) collective-permute-start(bf16[64,1152]{1,0:T(8,128)(2,1)S(1)} %convert_element_type.43), channel_id=1, source_target_pairs={{0,2},{2,4},{4,6},{6,0},{1,3},{3,5},{5,7},{7,1},{8,10},{10,12},{12... | collective-permute-start | bytes 442376 | tf_op jit(solution)/shard_map/ppermute | solution.py:1399
  29.5 20.4 %collective-permute-start.5 = (bf16[64,1152]{1,0:T(8,128)(2,1)S(1)}, bf16[64,1152]{1,0:T(8,128)(2,1)S(1)}, u32[]{:S(2)}, u32[]{:S(2)}) collective-permute-start(bf16[64,1152]{1,0:T(8,128)(2,1)S(1)} %convert_element_type.43), channel_id=1, source_target_pairs={{0,4},{2,6},{4,0},{6,2},{1,5},{3,7},{5,1},{7,3},{8,12},{10,14},{12... | collective-permute-start | bytes 442376 | tf_op jit(solution)/shard_map/ppermute | solution.py:1399
  31.1 18.8 %collective-permute-start.6 = (bf16[64,1152]{1,0:T(8,128)(2,1)S(1)}, bf16[64,1152]{1,0:T(8,128)(2,1)S(1)}, u32[]{:S(2)}, u32[]{:S(2)}) collective-permute-start(bf16[64,1152]{1,0:T(8,128)(2,1)S(1)} %convert_element_type.43), channel_id=1, source_target_pairs={{0,6},{2,0},{4,2},{6,4},{1,7},{3,1},{5,3},{7,5},{8,14},{10,8},{12,... | collective-permute-start | bytes 442376 | tf_op jit(solution)/shard_map/ppermute | solution.py:1399
  50.0 41.9 %all-to-all-start = ((bf16[8,390,2,128]{3,2,1,0:T(2,128)(2,1)}), bf16[8,390,2,128]{3,2,1,0:T(2,128)(2,1)S(1)}, u32[]{:S(2)}, u32[]{:S(2)}) async-start(bf16[8,390,2,128]{3,2,1,0:T(2,128)(2,1)} %get-tuple-element.95), calls=%async_computation | async-start | bytes 3194880 | tf_op jit(solution)/shard_map/all_to_all | solution.py:1476
  53.8 2.1 collective-permute-start.7
  91.8 38.2 %all-to-all-start.1 = ((bf16[8,696,128]{2,1,0:T(8,128)(2,1)}), bf16[8,696,128]{2,1,0:T(8,128)(2,1)S(1)}, u32[]{:S(2)}, u32[]{:S(2)}) async-start(bf16[8,696,128]{2,1,0:T(8,128)(2,1)} %get-tuple-element.96), calls=%async_computation.1 | async-start | bytes 2850816 | tf_op jit(solution)/shard_map/all_to_all | solution.py:1480
  113.7 11.5 %collective-permute-start.8 = (bf16[2,160,128]{2,1,0:T(8,128)(2,1)}, bf16[2,160,128]{2,1,0:T(8,128)(2,1)S(1)}, u32[]{:S(2)}, u32[]{:S(2)}) collective-permute-start(bf16[2,160,128]{2,1,0:T(8,128)(2,1)} %get-tuple-element.98), channel_id=1, source_target_pairs={{1,0},{2,1},{3,2},{4,3},{5,4},{6,5},{7,6},{9,8},{10,9},{11,10},{12... | collective-permute-start | bytes 245768 | tf_op jit(solution)/shard_map/ppermute | solution.py:29
  115.0 16.4 %collective-permute-start.9 = (bf16[2,160,128]{2,1,0:T(8,128)(2,1)}, bf16[2,160,128]{2,1,0:T(8,128)(2,1)S(1)}, u32[]{:S(2)}, u32[]{:S(2)}) collective-permute-start(bf16[2,160,128]{2,1,0:T(8,128)(2,1)} %get-tuple-element.103), channel_id=1, source_target_pairs={{0,1},{1,2},{2,3},{3,4},{4,5},{5,6},{6,7},{8,9},{9,10},{10,11},{11... | collective-permute-start | bytes 245768 | tf_op jit(solution)/shard_map/ppermute | solution.py:29
  143.9 2.1 collective-permute-start.10
  146.9 21.1 %all-to-all-start.2 = ((bf16[16,16,1152]{2,1,0:T(8,128)(2,1)}), bf16[16,16,1152]{2,1,0:T(8,128)(2,1)S(1)}, u32[]{:S(2)}, u32[]{:S(2)}) async-start(bf16[16,16,1152]{2,1,0:T(8,128)(2,1)} %bitcast.10), calls=%async_computation.2 | async-start | bytes 1179648 | tf_op jit(solution)/shard_map/all_to_all | solution.py:1435
  168.0 2.3 %collective-permute-start.11 = (bf16[256,1408]{1,0:T(8,128)(2,1)S(1)}, bf16[256,1408]{1,0:T(8,128)(2,1)}, u32[]{:S(2)}, u32[]{:S(2)}) collective-permute-start(bf16[256,1408]{1,0:T(8,128)(2,1)S(1)} %get-tuple-element.126), channel_id=1, source_target_pairs={{0,1},{1,0},{2,3},{3,2},{4,5},{5,4},{6,7},{7,6},{8,9},{9,8},{10,11... | collective-permute-start | bytes 2162696 | tf_op jit(solution)/shard_map/ppermute | solution.py:1399
  172.5 1.3 collective-permute-start.12
  174.0 12.1 %collective-permute-start.13 = (f32[2,5,2,256]{3,2,1,0:T(2,128)S(1)}, f32[2,5,2,256]{3,2,1,0:T(2,128)S(1)}, u32[]{:S(2)}, u32[]{:S(2)}) collective-permute-start(f32[2,5,2,256]{3,2,1,0:T(2,128)S(1)} %get-tuple-element.159), channel_id=1, source_target_pairs={{0,6},{2,0},{4,2},{6,4},{1,7},{3,1},{5,3},{7,5},{8,14},{10,8},{12,... | collective-permute-start | bytes 61448 | tf_op jit(solution)/shard_map/ppermute | solution.py:1399
  175.8 24.7 %all-to-all-start.3 = ((bf16[16,16,1408]{2,1,0:T(8,128)(2,1)}), bf16[16,16,1408]{2,1,0:T(8,128)(2,1)S(1)}, u32[]{:S(2)}, u32[]{:S(2)}) async-start(bf16[16,16,1408]{2,1,0:T(8,128)(2,1)} %bitcast.29), calls=%async_computation.3 | async-start | bytes 1441792 | tf_op jit(solution)/shard_map/all_to_all | solution.py:1435
  181.7 22.7 %copy-start.30 = (f32[224]{0:T(256)S(1)}, f32[224]{0:T(256)}, u32[]{:S(2)}) copy-start(f32[224]{0:T(256)} %param.33) | copy-start | bytes 2692
  181.7 17.8 %collective-permute-start.14 = (f32[2,5,2,256]{3,2,1,0:T(2,128)S(1)}, f32[2,5,2,256]{3,2,1,0:T(2,128)S(1)}, u32[]{:S(2)}, u32[]{:S(2)}) collective-permute-start(f32[2,5,2,256]{3,2,1,0:T(2,128)S(1)} %get-tuple-element.160), channel_id=1, source_target_pairs={{0,4},{2,6},{4,0},{6,2},{1,5},{3,7},{5,1},{7,3},{8,12},{10,14},{12... | collective-permute-start | bytes 61448 | tf_op jit(solution)/shard_map/ppermute | solution.py:1399
  184.6 15.0 %collective-permute-start.15 = (f32[2,5,2,256]{3,2,1,0:T(2,128)S(1)}, f32[2,5,2,256]{3,2,1,0:T(2,128)S(1)}, u32[]{:S(2)}, u32[]{:S(2)}) collective-permute-start(f32[2,5,2,256]{3,2,1,0:T(2,128)S(1)} %get-tuple-element.158), channel_id=1, source_target_pairs={{0,2},{2,4},{4,6},{6,0},{1,3},{3,5},{5,7},{7,1},{8,10},{10,12},{12... | collective-permute-start | bytes 61448 | tf_op jit(solution)/shard_map/ppermute | solution.py:1399
  200.7 4.5 %collective-permute-start.16 = (bf16[16,2560]{1,0:T(8,128)(2,1)S(1)}, bf16[16,2560]{1,0:T(8,128)(2,1)S(1)}, u32[]{:S(2)}, u32[]{:S(2)}) collective-permute-start(bf16[16,2560]{1,0:T(8,128)(2,1)S(1)} %get-tuple-element.156), channel_id=1, source_target_pairs={{0,24},{8,0},{16,8},{24,16},{1,25},{9,1},{17,9},{25,17},{2,26},{10... | collective-permute-start | bytes 245768 | tf_op jit(solution)/shard_map/ppermute | solution.py:1399
  203.1 4.7 %collective-permute-start.17 = (bf16[16,2560]{1,0:T(8,128)(2,1)S(1)}, bf16[16,2560]{1,0:T(8,128)(2,1)S(1)}, u32[]{:S(2)}, u32[]{:S(2)}) collective-permute-start(bf16[16,2560]{1,0:T(8,128)(2,1)S(1)} %get-tuple-element.156), channel_id=1, source_target_pairs={{0,16},{8,24},{16,0},{24,8},{1,17},{9,25},{17,1},{25,9},{2,18},{10... | collective-permute-start | bytes 245768 | tf_op jit(solution)/shard_map/ppermute | solution.py:1399
  203.7 5.3 %collective-permute-start.18 = (bf16[16,2560]{1,0:T(8,128)(2,1)S(1)}, bf16[16,2560]{1,0:T(8,128)(2,1)S(1)}, u32[]{:S(2)}, u32[]{:S(2)}) collective-permute-start(bf16[16,2560]{1,0:T(8,128)(2,1)S(1)} %get-tuple-element.156), channel_id=1, source_target_pairs={{0,8},{8,16},{16,24},{24,0},{1,9},{9,17},{17,25},{25,1},{2,10},{10... | collective-permute-start | bytes 245768 | tf_op jit(solution)/shard_map/ppermute | solution.py:1399
  (32 other events, 262.5 us)
